TPU v7x, 32 devices: a whole 2x2x4 slice. The times are simulated.
32 devices in a mesh: spec: 4 (over y, core), pix: 8 (over z, x).
Axes of the slice: x: 2, y: 2, z: 4, core: 2. Of those that a mesh axis runs over, the one named last changes fastest.
Arguments:
- spectra_flux: float32 [768, 4096], P('spec', 'pix'), may hold values from -8 to 8
- pixel_weights: float32 [768, 4096], P('spec', 'pix'), may hold values from 0.05 to 20
- old_basis: float32 [32, 4096], P(None, 'pix'), may hold values from -3 to 3
Outputs:
- new_basis: float32 [32, 4096], P(None, 'pix')
All inputs are finite; a program needn't handle non-finite values.
Results may differ from a plain program's by a relative error of at most 0.0003.
Values sent between devices are 32-bit elements; how exact they have to be, the bound alone decides.
No kernel may reach another device: no remote copies, remote signals or barrier semaphores. Data moves between devices by JAX's collectives and lax.ppermute only.
A program may use at most 64 MiB of HBM per device.

v0:
```python
import functools

import jax
import jax.numpy as jnp
from jax import lax
from jax.experimental import pallas as pl
from jax.experimental.pallas import tpu as pltpu
from jax.sharding import PartitionSpec as P

LANES = 128
ROWS = 8
VMEM = pl.BlockSpec(memory_space=pltpu.VMEM)
SMEM = pl.BlockSpec(memory_space=pltpu.SMEM)
LIMIT = 48 * 1024 * 1024


def up(value, multiple):
    return -(-value // multiple) * multiple


def pair_rows(rank):
    return rank * (rank // 2) + rank // 2


def write_pairs(twice, pairs, rank):
    first = twice[0:rank, :]
    for diag in range(rank // 2):
        pairs[diag * rank : (diag + 1) * rank, :] = first * twice[diag : diag + rank, :]
    half = rank // 2
    pairs[half * rank : half * rank + half, :] = first[0:half] * first[half:rank]


def unpack(packed, full, rank):
    for diag in range(rank // 2 + 1):
        base = diag * rank
        count = rank if diag < rank // 2 else rank // 2
        wrap = min(count, rank - diag)
        part = packed[base : base + wrap, :]
        full[pl.ds(diag, wrap, stride=rank + 1), :] = part
        if diag:
            full[pl.ds(diag * rank, wrap, stride=rank + 1), :] = part
        if wrap < count:
            part = packed[base + wrap : base + count, :]
            full[pl.ds(rank - diag, count - wrap, stride=rank + 1), :] = part
            full[pl.ds((rank - diag) * rank, count - wrap, stride=rank + 1), :] = part


def solve(full, target, scaled, rank):
    row = lax.broadcasted_iota(jnp.int32, target.shape, 0)
    pivots = jnp.zeros_like(target)
    for k in range(rank):
        column = full[k * rank : (k + 1) * rank, :]
        for j in range(k):
            column = column - scaled[j * rank : (j + 1) * rank, :] * full[j * rank + k : j * rank + k + 1, :]
        full[k * rank : (k + 1) * rank, :] = column
        here = row == k
        factor = jnp.where(here, 0.0, column * (1.0 / column[k : k + 1, :]))
        scaled[k * rank : (k + 1) * rank, :] = factor
        pivots = jnp.where(here, column, pivots)
        target = target - factor * target[k : k + 1, :]
    return target / pivots


def dot(left, right, right_axis):
    return lax.dot_general(
        left,
        right,
        (((1,), (right_axis,)), ((), ())),
        precision=lax.Precision.HIGHEST,
        preferred_element_type=jnp.float32,
    )


def spec_kernel(me, flux, weights, basis, gram, *rest, peers, chunk):
    picks, (twice, pairs) = rest[:peers], rest[peers:]
    rank, pixels = basis.shape
    share = pixels // peers
    lead = pair_rows(rank)
    twice[0:rank, :] = basis[...]
    twice[rank:, :] = basis[...]
    write_pairs(twice, pairs, rank)
    weighted = weights[...] * flux[...]
    packed = dot(weights[...], pairs[...], 1)
    target = dot(weighted, basis[...], 1)
    for k in range(gram.shape[0]):
        gram[k, 0:chunk, 0:lead] = packed[k * chunk : (k + 1) * chunk, :]
        gram[k, 0:chunk, lead : lead + rank] = target[k * chunk : (k + 1) * chunk, :]
    for q in range(peers):
        start = (me[0] ^ q) * share
        if share % LANES == 0:
            start = pl.multiple_of(start, LANES)
            picks[q][0] = weights[:, pl.ds(start, share)]
            picks[q][1] = weights[:, pl.ds(start, share)] * flux[:, pl.ds(start, share)]
        else:
            for s in range(peers):

                @pl.when(me[0] ^ q == s)
                def _():
                    picks[q][0] = weights[:, s * share : (s + 1) * share]
                    picks[q][1] = weighted[:, s * share : (s + 1) * share]


def coeff_kernel(parts, out, packed, full, scaled, *, rank, chunk):
    total = parts[0]
    for k in range(1, parts.shape[0]):
        total = total + parts[k]
    rows = total.shape[0]
    square = jnp.concatenate([total, jnp.ones((LANES - rows, total.shape[1]), jnp.float32)], axis=0)
    for k in range(total.shape[1] // LANES):
        packed[k * LANES : (k + 1) * LANES, :] = square[:, k * LANES : (k + 1) * LANES].T
    lead = pair_rows(rank)
    unpack(packed, full, rank)
    solved = solve(full, packed[lead : lead + rank, :], scaled, rank)
    lane = lax.broadcasted_iota(jnp.int32, (ROWS, LANES), 1)
    tile = jnp.zeros((ROWS, LANES), jnp.float32)
    for a in range(rank // ROWS):
        part = solved[a * ROWS : (a + 1) * ROWS, :]
        if a:
            part = pltpu.roll(part, a * chunk, 1)
        tile = jnp.where((lane >= a * chunk) & (lane < (a + 1) * chunk), part, tile)
    for k in range(out.shape[0]):
        out[k] = tile


def pixel_kernel(me, tiles, *rest, peers, rank, chunk):
    picks, (out, twice, pairs, both, full, scaled) = rest[:peers], rest[peers:]
    spectra = picks[0].shape[1]
    share = picks[0].shape[2]
    group = spectra // chunk
    lane = lax.broadcasted_iota(jnp.int32, (ROWS, LANES), 1)
    width = twice.shape[1]
    for q in range(peers):
        both[0, q * spectra : (q + 1) * spectra, :] = picks[q][0]
        both[1, q * spectra : (q + 1) * spectra, :] = picks[q][1]
    for a in range(rank // ROWS):
        columns = [jnp.zeros((ROWS, LANES), jnp.float32) for _ in range(width // LANES)]
        for q in range(peers):
            for k in range(group):
                part = tiles[(me[0] ^ q) * group + k]
                start = q * spectra + k * chunk
                shift = (start - a * chunk) % LANES
                if shift:
                    part = pltpu.roll(part, shift, 1)
                for t in range(start // LANES, (start + chunk - 1) // LANES + 1):
                    low, high = max(start - t * LANES, 0), min(start + chunk - t * LANES, LANES)
                    columns[t] = jnp.where((lane >= low) & (lane < high), part, columns[t])
        for t, column in enumerate(columns):
            twice[a * ROWS : (a + 1) * ROWS, t * LANES : (t + 1) * LANES] = column
            twice[rank + a * ROWS : rank + (a + 1) * ROWS, t * LANES : (t + 1) * LANES] = column
    write_pairs(twice, pairs, rank)
    depth = both.shape[1]
    packed = dot(pairs[:, 0:depth], both[0], 0)
    target = dot(twice[0:rank, 0:depth], both[1], 0)
    if share < LANES:
        filler = jnp.ones((packed.shape[0], LANES - share), jnp.float32)
        packed = jnp.concatenate([packed, filler], axis=1)
        target = jnp.concatenate([target, filler[0:rank]], axis=1)
    unpack(packed, full, rank)
    out[...] = solve(full, target, scaled, rank)[:, 0:share]


def place_kernel(me, *rest, peers):
    shares, out = rest[:peers], rest[peers]
    share = shares[0].shape[1]
    for q in range(peers):
        if share % LANES == 0:
            out[:, pl.ds(pl.multiple_of((me[0] ^ q) * share, LANES), share)] = shares[q][...]
        else:
            for s in range(peers):

                @pl.when(me[0] ^ q == s)
                def _():
                    out[:, s * share : (s + 1) * share] = shares[q][...]


def call(kernel, outs, scratch, *args, smem=0):
    return pl.pallas_call(
        kernel,
        out_shape=outs,
        in_specs=[SMEM] * smem + [VMEM] * (len(args) - smem),
        out_specs=jax.tree.map(lambda _: VMEM, outs),
        scratch_shapes=[pltpu.VMEM(shape, jnp.float32) for shape in scratch],
        compiler_params=pltpu.CompilerParams(vmem_limit_bytes=LIMIT),
    )(*args)


def shape(*sizes):
    return jax.ShapeDtypeStruct(sizes, jnp.float32)


def local(peers, groups, spectra_flux, pixel_weights, old_basis):
    spectra, pixels = pixel_weights.shape
    rank = old_basis.shape[0]
    share, chunk = pixels // peers, spectra // groups
    lead = pair_rows(rank)
    wide = up(lead + rank, LANES)
    me = lax.axis_index("spec").astype(jnp.int32).reshape(1)

    gram, *picks = call(
        functools.partial(spec_kernel, peers=peers, chunk=chunk),
        [shape(groups, up(chunk, ROWS), wide)] + [shape(2, spectra, share)] * peers,
        [(2 * rank, pixels), (lead, pixels)],
        me,
        spectra_flux,
        pixel_weights,
        old_basis,
        smem=1,
    )

    def swap(value, q):
        return lax.ppermute(value, "spec", [(s, s ^ q) for s in range(peers)])

    picks = [picks[0]] + [swap(picks[q], q) for q in range(1, peers)]
    parts = lax.all_to_all(gram, "pix", 0, 0)
    tiles = call(
        functools.partial(coeff_kernel, rank=rank, chunk=chunk),
        shape(peers * groups, ROWS, LANES),
        [(wide, LANES), (rank * rank, LANES), (rank * rank, LANES)],
        parts,
    )
    tiles = lax.all_to_all(tiles, ("spec", "pix"), 0, 0)
    depth = peers * spectra
    basis_share = call(
        functools.partial(pixel_kernel, peers=peers, rank=rank, chunk=chunk),
        shape(rank, share),
        [
            (2 * rank, up(depth, LANES)),
            (lead, up(depth, LANES)),
            (2, depth, share),
            (rank * rank, LANES),
            (rank * rank, LANES),
        ],
        me,
        tiles,
        *picks,
        smem=1,
    )
    shares = [basis_share] + [swap(basis_share, q) for q in range(1, peers)]
    return call(functools.partial(place_kernel, peers=peers), shape(rank, pixels), [], me, *shares, smem=1)


def solution(mesh):
    placed = (P("spec", "pix"), P("spec", "pix"), P(None, "pix"))
    body = functools.partial(local, mesh.shape["spec"], mesh.shape["pix"])
    return jax.shard_map(body, mesh=mesh, in_specs=placed, out_specs=P(None, "pix"), check_vma=False)
```

profile of v0, /device:TPU:0, one launch (start us, length us, event | category | flops | bytes accessed | tf_op | source)
XLA Modules:
  0.0 51.4 jit_solution(14289126061751320456)
XLA Ops:
  0.0 0.0 copy-start
  0.0 1.0 %copy-done = f32[192,512]{1,0:T(8,128)S(1)} copy-done((f32[192,512]{1,0:T(8,128)S(1)}, f32[192,512]{1,0:T(8,128)}, u32[]{:S(2)}) %copy-start) | copy-done | bytes 393240
  1.0 0.0 copy-start.1
  1.0 1.0 %copy-done.1 = f32[192,512]{1,0:T(8,128)S(1)} copy-done((f32[192,512]{1,0:T(8,128)S(1)}, f32[192,512]{1,0:T(8,128)}, u32[]{:S(2)}) %copy-start.1) | copy-done | bytes 393240
  2.0 0.0 copy-start.2
  2.0 0.8 %copy-done.2 = f32[32,512]{1,0:T(8,128)S(1)} copy-done((f32[32,512]{1,0:T(8,128)S(1)}, f32[32,512]{1,0:T(8,128)}, u32[]{:S(2)}) %copy-start.2) | copy-done | bytes 65560
  2.8 1.9 %shard_map.37 = (f32[8,24,640]{2,1,0:T(8,128)S(1)}, f32[2,192,128]{2,1,0:T(8,128)S(1)}, f32[2,192,128]{2,1,0:T(8,128)S(1)}, f32[2,192,128]{2,1,0:T(8,128)S(1)}, f32[2,192,128]{2,1,0:T(8,128)S(1)}) custom-call(s32[1]{0:T(128)} %bitcast.me, f32[192,512]{1,0:T(8,128)S(1)} %copy-done, f32[192,512]{1,0:T(8,128)S(1)} %copy-done.1, f32[32,512]{1,0:T(8,128)S(1)} %copy-done.2), custom_call_target="tpu_custom_call" | custom-call | tf_op jit(solution)/shard_map/pallas_call | solution.py:177
  4.8 20.9 %all_to_all.10.parts = f32[8,24,640]{2,1,0:T(8,128)S(1)} all-to-all(f32[8,24,640]{2,1,0:T(8,128)S(1)} %get-tuple-element.10), channel_id=1, replica_groups=mesh['spec'=4,'pix'=8] {'pix'}, dimensions={0} | all-to-all | bytes 983040 | tf_op jit(solution)/shard_map/all_to_all | solution.py:214
  25.7 1.4 %shard_map.38 = f32[32,8,128]{2,1,0:T(8,128)} custom-call(f32[8,24,640]{2,1,0:T(8,128)S(1)} %all_to_all.10.parts), custom_call_target="tpu_custom_call" | custom-call | tf_op jit(solution)/shard_map/pallas_call | solution.py:177
  27.1 3.6 %all-to-all-start.1 = ((f32[32,8,128]{2,1,0:T(8,128)}), f32[32,8,128]{2,1,0:T(8,128)S(1)}, u32[]{:S(2)}, u32[]{:S(2)}) async-start(f32[32,8,128]{2,1,0:T(8,128)} %shard_map.38), calls=%async_computation.1 | async-start | bytes 262144 | tf_op jit(solution)/shard_map/all_to_all | solution.py:221
  30.7 0.3 collective-permute-start
  31.1 1.7 %collective-permute-start.1 = (f32[2,192,128]{2,1,0:T(8,128)S(1)}, f32[2,192,128]{2,1,0:T(8,128)S(1)}, u32[]{:S(2)}, u32[]{:S(2)}) collective-permute-start(f32[2,192,128]{2,1,0:T(8,128)S(1)} %get-tuple-element.13), channel_id=1, source_target_pairs={{0,16},{8,24},{16,0},{24,8},{1,17},{9,25},{17,1},{25,9},{2,18},{10... | collective-permute-start | bytes 589832 | tf_op jit(solution)/shard_map/ppermute | solution.py:211
  32.7 0.0 collective-permute-start.2
  32.8 0.0 collective-permute-done.rest_1_
  32.8 7.3 %collective-permute-done.1.rest_2_ = f32[2,192,128]{2,1,0:T(8,128)S(1)} collective-permute-done((f32[2,192,128]{2,1,0:T(8,128)S(1)}, f32[2,192,128]{2,1,0:T(8,128)S(1)}, u32[]{:S(2)}, u32[]{:S(2)}) %collective-permute-start.1) | collective-permute-done | bytes 196640 | tf_op jit(solution)/shard_map/ppermute | solution.py:211
  40.0 3.1 %collective-permute-done.2.rest_3_ = f32[2,192,128]{2,1,0:T(8,128)S(1)} collective-permute-done((f32[2,192,128]{2,1,0:T(8,128)S(1)}, f32[2,192,128]{2,1,0:T(8,128)S(1)}, u32[]{:S(2)}, u32[]{:S(2)}) %collective-permute-start.2) | collective-permute-done | bytes 196640 | tf_op jit(solution)/shard_map/ppermute | solution.py:211
  43.1 0.0 all-to-all-done.1.tiles
  43.1 2.4 %shard_map.39.rest_0_ = f32[32,128]{1,0:T(8,128)S(1)} custom-call(s32[1]{0:T(128)} %bitcast.me, f32[32,8,128]{2,1,0:T(8,128)S(1)} %all-to-all-done.1.tiles, f32[2,192,128]{2,1,0:T(8,128)S(1)} %get-tuple-element.11.rest_0_, f32[2,192,128]{2,1,0:T(8,128)S(1)} %collective-permute-done.rest_1_, f32[2,192,128]{2,1,0:T(8,128)S(1)} %collective-permute-done.1.rest_2_, ...), custom_call_target="tpu_custom_call" | custom-call | tf_op jit(solution)/shard_map/pallas_call | solution.py:177
  45.5 1.5 %collective-permute-start.5 = (f32[32,128]{1,0:T(8,128)S(1)}, f32[32,128]{1,0:T(8,128)S(1)}, u32[]{:S(2)}, u32[]{:S(2)}) collective-permute-start(f32[32,128]{1,0:T(8,128)S(1)} %shard_map.39.rest_0_), channel_id=1, source_target_pairs={{0,24},{8,16},{16,8},{24,0},{1,25},{9,17},{17,9},{25,1},{2,26},{10... | collective-permute-start | bytes 49160 | tf_op jit(solution)/shard_map/ppermute | solution.py:211
  47.0 0.6 %collective-permute-start.4 = (f32[32,128]{1,0:T(8,128)S(1)}, f32[32,128]{1,0:T(8,128)S(1)}, u32[]{:S(2)}, u32[]{:S(2)}) collective-permute-start(f32[32,128]{1,0:T(8,128)S(1)} %shard_map.39.rest_0_), channel_id=1, source_target_pairs={{0,16},{8,24},{16,0},{24,8},{1,17},{9,25},{17,1},{25,9},{2,18},{10... | collective-permute-start | bytes 49160 | tf_op jit(solution)/shard_map/ppermute | solution.py:211
  47.6 0.0 collective-permute-start.3
  47.6 1.2 %collective-permute-done.5.rest_3_ = f32[32,128]{1,0:T(8,128)S(1)} collective-permute-done((f32[32,128]{1,0:T(8,128)S(1)}, f32[32,128]{1,0:T(8,128)S(1)}, u32[]{:S(2)}, u32[]{:S(2)}) %collective-permute-start.5) | collective-permute-done | bytes 16416 | tf_op jit(solution)/shard_map/ppermute | solution.py:211
  48.8 2.0 %collective-permute-done.4.rest_2_ = f32[32,128]{1,0:T(8,128)S(1)} collective-permute-done((f32[32,128]{1,0:T(8,128)S(1)}, f32[32,128]{1,0:T(8,128)S(1)}, u32[]{:S(2)}, u32[]{:S(2)}) %collective-permute-start.4) | collective-permute-done | bytes 16416 | tf_op jit(solution)/shard_map/ppermute | solution.py:211
  50.8 0.0 collective-permute-done.3.rest_1_
  50.8 0.6 %shard_map.40 = f32[32,512]{1,0:T(8,128)} custom-call(s32[1]{0:T(128)} %bitcast.me, f32[32,128]{1,0:T(8,128)S(1)} %shard_map.39.rest_0_, f32[32,128]{1,0:T(8,128)S(1)} %collective-permute-done.3.rest_1_, f32[32,128]{1,0:T(8,128)S(1)} %collective-permute-done.4.rest_2_, f32[32,128]{1,0:T(8,128)S(1)} %collective-permute-done.5.rest_3_), custom_call_target="tpu_custom_call" | custom-call | tf_op jit(solution)/shard_map/pallas_call | solution.py:177
Async XLA Ops:
  0.0 1.0 %copy-start = (f32[192,512]{1,0:T(8,128)S(1)}, f32[192,512]{1,0:T(8,128)}, u32[]{:S(2)}) copy-start(f32[192,512]{1,0:T(8,128)} %flux.1) | copy-start | bytes 1179652
  1.0 1.0 %copy-start.1 = (f32[192,512]{1,0:T(8,128)S(1)}, f32[192,512]{1,0:T(8,128)}, u32[]{:S(2)}) copy-start(f32[192,512]{1,0:T(8,128)} %weights.1) | copy-start | bytes 1179652
  2.0 0.8 %copy-start.2 = (f32[32,512]{1,0:T(8,128)S(1)}, f32[32,512]{1,0:T(8,128)}, u32[]{:S(2)}) copy-start(f32[32,512]{1,0:T(8,128)} %basis.1) | copy-start | bytes 196612
  27.1 16.0 %all-to-all-start.1 = ((f32[32,8,128]{2,1,0:T(8,128)}), f32[32,8,128]{2,1,0:T(8,128)S(1)}, u32[]{:S(2)}, u32[]{:S(2)}) async-start(f32[32,8,128]{2,1,0:T(8,128)} %shard_map.38), calls=%async_computation.1 | async-start | bytes 262144 | tf_op jit(solution)/shard_map/all_to_all | solution.py:221
  30.7 2.0 %collective-permute-start = (f32[2,192,128]{2,1,0:T(8,128)S(1)}, f32[2,192,128]{2,1,0:T(8,128)S(1)}, u32[]{:S(2)}, u32[]{:S(2)}) collective-permute-start(f32[2,192,128]{2,1,0:T(8,128)S(1)} %get-tuple-element.12), channel_id=1, source_target_pairs={{0,8},{8,0},{16,24},{24,16},{1,9},{9,1},{17,25},{25,17},{2,10},{10... | collective-permute-start | bytes 589832 | tf_op jit(solution)/shard_map/ppermute | solution.py:211
  31.1 8.9 %collective-permute-start.1 = (f32[2,192,128]{2,1,0:T(8,128)S(1)}, f32[2,192,128]{2,1,0:T(8,128)S(1)}, u32[]{:S(2)}, u32[]{:S(2)}) collective-permute-start(f32[2,192,128]{2,1,0:T(8,128)S(1)} %get-tuple-element.13), channel_id=1, source_target_pairs={{0,16},{8,24},{16,0},{24,8},{1,17},{9,25},{17,1},{25,9},{2,18},{10... | collective-permute-start | bytes 589832 | tf_op jit(solution)/shard_map/ppermute | solution.py:211
  32.7 10.4 %collective-permute-start.2 = (f32[2,192,128]{2,1,0:T(8,128)S(1)}, f32[2,192,128]{2,1,0:T(8,128)S(1)}, u32[]{:S(2)}, u32[]{:S(2)}) collective-permute-start(f32[2,192,128]{2,1,0:T(8,128)S(1)} %get-tuple-element.14), channel_id=1, source_target_pairs={{0,24},{8,16},{16,8},{24,0},{1,25},{9,17},{17,9},{25,1},{2,26},{10... | collective-permute-start | bytes 589832 | tf_op jit(solution)/shard_map/ppermute | solution.py:211
  45.5 3.2 %collective-permute-start.5 = (f32[32,128]{1,0:T(8,128)S(1)}, f32[32,128]{1,0:T(8,128)S(1)}, u32[]{:S(2)}, u32[]{:S(2)}) collective-permute-start(f32[32,128]{1,0:T(8,128)S(1)} %shard_map.39.rest_0_), channel_id=1, source_target_pairs={{0,24},{8,16},{16,8},{24,0},{1,25},{9,17},{17,9},{25,1},{2,26},{10... | collective-permute-start | bytes 49160 | tf_op jit(solution)/shard_map/ppermute | solution.py:211
  47.0 3.8 %collective-permute-start.4 = (f32[32,128]{1,0:T(8,128)S(1)}, f32[32,128]{1,0:T(8,128)S(1)}, u32[]{:S(2)}, u32[]{:S(2)}) collective-permute-start(f32[32,128]{1,0:T(8,128)S(1)} %shard_map.39.rest_0_), channel_id=1, source_target_pairs={{0,16},{8,24},{16,0},{24,8},{1,17},{9,25},{17,1},{25,9},{2,18},{10... | collective-permute-start | bytes 49160 | tf_op jit(solution)/shard_map/ppermute | solution.py:211
  47.6 3.2 %collective-permute-start.3 = (f32[32,128]{1,0:T(8,128)S(1)}, f32[32,128]{1,0:T(8,128)S(1)}, u32[]{:S(2)}, u32[]{:S(2)}) collective-permute-start(f32[32,128]{1,0:T(8,128)S(1)} %shard_map.39.rest_0_), channel_id=1, source_target_pairs={{0,8},{8,0},{16,24},{24,16},{1,9},{9,1},{17,25},{25,17},{2,10},{10... | collective-permute-start | bytes 49160 | tf_op jit(solution)/shard_map/ppermute | solution.py:211
where the time goes:
time: 51.7 us; the launch traced here: 51.4 us
  blocking collectives  20.9 us (40%)
  waiting for transfers between devices  13.6 us (26%)
  starting transfers between devices  7.7 us (15%)
  Pallas kernels  6.4 us (12%)
  local copies, waits for them, and re-layouts  2.83 us (5%)
    all_to_all x1, blocking collectives, local(): parts = lax.all_to_all(gram, 'pix', 0, 0)  20.9 us
    ppermute x6, waiting for transfers between devices, swap(): return lax.ppermute(value, 'spec', [(s, s ^ q) for s in range(peers)])  13.6 us
    pallas_call x4, Pallas kernels, call(): pl.pallas_call(kernel, out_shape=outs, in_specs=[SMEM] * smem + [VMEM] *...  6.4 us
    ppermute x6, starting transfers between devices, swap(): return lax.ppermute(value, 'spec', [(s, s ^ q) for s in range(peers)])  4.07 us
    all_to_all x1, starting transfers between devices, local(): tiles = lax.all_to_all(tiles, ('spec', 'pix'), 0, 0)  3.64 us
    unnamed x6, local copies, waits for them, and re-layouts  2.83 us
  transfers between devices with their start and end apart: 7, of which 4 were waited for; matrix products, arithmetic and copies ran while one was open for 0% of the time, Pallas kernels for 0%

commit v1 on v0

--- a/solution.py
+++ b/solution.py
@@ -10,7 +10,6 @@
 LANES = 128
 ROWS = 8
 VMEM = pl.BlockSpec(memory_space=pltpu.VMEM)
-SMEM = pl.BlockSpec(memory_space=pltpu.SMEM)
 LIMIT = 48 * 1024 * 1024
 
 
@@ -71,39 +70,50 @@
     )
 
 
-def spec_kernel(me, flux, weights, basis, gram, *rest, peers, chunk):
-    picks, (twice, pairs) = rest[:peers], rest[peers:]
+def spec_kernel(flux_hbm, weights_hbm, basis_hbm, keep, send, own, other, *scratch, chunk):
+    flux, weights, basis, twice, pairs, grams, sems = scratch
+    copies = [
+        pltpu.make_async_copy(source, target, sems.at[k])
+        for k, (source, target) in enumerate(((basis_hbm, basis), (weights_hbm, weights), (flux_hbm, flux)))
+    ]
+    for copy in copies:
+        copy.start()
     rank, pixels = basis.shape
-    share = pixels // peers
+    half = own.shape[2]
     lead = pair_rows(rank)
+    copies[0].wait()
     twice[0:rank, :] = basis[...]
     twice[rank:, :] = basis[...]
     write_pairs(twice, pairs, rank)
-    weighted = weights[...] * flux[...]
+    copies[1].wait()
     packed = dot(weights[...], pairs[...], 1)
-    target = dot(weighted, basis[...], 1)
-    for k in range(gram.shape[0]):
-        gram[k, 0:chunk, 0:lead] = packed[k * chunk : (k + 1) * chunk, :]
-        gram[k, 0:chunk, lead : lead + rank] = target[k * chunk : (k + 1) * chunk, :]
-    for q in range(peers):
-        start = (me[0] ^ q) * share
-        if share % LANES == 0:
-            start = pl.multiple_of(start, LANES)
-            picks[q][0] = weights[:, pl.ds(start, share)]
-            picks[q][1] = weights[:, pl.ds(start, share)] * flux[:, pl.ds(start, share)]
-        else:
-            for s in range(peers):
-
-                @pl.when(me[0] ^ q == s)
-                def _():
-                    picks[q][0] = weights[:, s * share : (s + 1) * share]
-                    picks[q][1] = weighted[:, s * share : (s + 1) * share]
-
-
-def coeff_kernel(parts, out, packed, full, scaled, *, rank, chunk):
-    total = parts[0]
-    for k in range(1, parts.shape[0]):
-        total = total + parts[k]
+    copies[2].wait()
+    flux[...] = weights[...] * flux[...]
+    target = dot(flux[...], basis[...], 1)
+    for k in range(grams.shape[0]):
+        grams[k, 0:chunk, 0:lead] = packed[k * chunk : (k + 1) * chunk, :]
+        grams[k, 0:chunk, lead : lead + rank] = target[k * chunk : (k + 1) * chunk, :]
+    for k in range(grams.shape[0] // 2):
+        keep[k] = grams[lax.axis_index("pix") ^ (2 * k)]
+        send[k] = grams[lax.axis_index("pix") ^ (2 * k + 1)]
+    low = pl.multiple_of((lax.axis_index("spec") & 1) * half, LANES)
+    high = pl.multiple_of(half - low, LANES)
+    own[0] = weights[:, pl.ds(low, half)]
+    own[1] = flux[:, pl.ds(low, half)]
+    other[0] = weights[:, pl.ds(high, half)]
+    other[1] = flux[:, pl.ds(high, half)]
+
+
+def fold_kernel(keep, arrived, *outs):
+    for k, out in enumerate(outs):
+        out[...] = keep[k] + arrived[k]
+
+
+def coeff_kernel(*refs, rank, chunk):
+    parts, (out, packed, full, scaled) = refs[:-4], refs[-4:]
+    total = parts[0][...]
+    for part in parts[1:]:
+        total = total + part[...]
     rows = total.shape[0]
     square = jnp.concatenate([total, jnp.ones((LANES - rows, total.shape[1]), jnp.float32)], axis=0)
     for k in range(total.shape[1] // LANES):
@@ -122,10 +132,10 @@
         out[k] = tile
 
 
-def pixel_kernel(me, tiles, *rest, peers, rank, chunk):
+def pixel_kernel(tiles, *rest, peers, rank, chunk):
     picks, (out, twice, pairs, both, full, scaled) = rest[:peers], rest[peers:]
     spectra = picks[0].shape[1]
-    share = picks[0].shape[2]
+    half = picks[0].shape[2]
     group = spectra // chunk
     lane = lax.broadcasted_iota(jnp.int32, (ROWS, LANES), 1)
     width = twice.shape[1]
@@ -136,7 +146,7 @@
         columns = [jnp.zeros((ROWS, LANES), jnp.float32) for _ in range(width // LANES)]
         for q in range(peers):
             for k in range(group):
-                part = tiles[(me[0] ^ q) * group + k]
+                part = tiles[(lax.axis_index("spec") ^ q) * group + k]
                 start = q * spectra + k * chunk
                 shift = (start - a * chunk) % LANES
                 if shift:
@@ -151,35 +161,28 @@
     depth = both.shape[1]
     packed = dot(pairs[:, 0:depth], both[0], 0)
     target = dot(twice[0:rank, 0:depth], both[1], 0)
-    if share < LANES:
-        filler = jnp.ones((packed.shape[0], LANES - share), jnp.float32)
-        packed = jnp.concatenate([packed, filler], axis=1)
-        target = jnp.concatenate([target, filler[0:rank]], axis=1)
-    unpack(packed, full, rank)
-    out[...] = solve(full, target, scaled, rank)[:, 0:share]
-
-
-def place_kernel(me, *rest, peers):
-    shares, out = rest[:peers], rest[peers]
-    share = shares[0].shape[1]
-    for q in range(peers):
-        if share % LANES == 0:
-            out[:, pl.ds(pl.multiple_of((me[0] ^ q) * share, LANES), share)] = shares[q][...]
-        else:
-            for s in range(peers):
-
-                @pl.when(me[0] ^ q == s)
-                def _():
-                    out[:, s * share : (s + 1) * share] = shares[q][...]
-
-
-def call(kernel, outs, scratch, *args, smem=0):
+    for t in range(half // LANES):
+        lanes = slice(t * LANES, (t + 1) * LANES)
+        unpack(packed[:, lanes], full.at[t], rank)
+    for t in range(half // LANES):
+        lanes = slice(t * LANES, (t + 1) * LANES)
+        out[:, lanes] = solve(full.at[t], target[:, lanes], scaled.at[t], rank)
+
+
+def place_kernel(own, other, out):
+    half = own.shape[1]
+    low = pl.multiple_of((lax.axis_index("spec") & 1) * half, LANES)
+    out[:, pl.ds(low, half)] = own[...]
+    out[:, pl.ds(pl.multiple_of(half - low, LANES), half)] = other[...]
+
+
+def call(kernel, outs, scratch, *args, space=pltpu.VMEM):
     return pl.pallas_call(
         kernel,
         out_shape=outs,
-        in_specs=[SMEM] * smem + [VMEM] * (len(args) - smem),
+        in_specs=[pl.BlockSpec(memory_space=space)] * len(args),
         out_specs=jax.tree.map(lambda _: VMEM, outs),
-        scratch_shapes=[pltpu.VMEM(shape, jnp.float32) for shape in scratch],
+        scratch_shapes=[pltpu.VMEM(s, jnp.float32) if isinstance(s, tuple) else s for s in scratch],
         compiler_params=pltpu.CompilerParams(vmem_limit_bytes=LIMIT),
     )(*args)
 
@@ -191,52 +194,56 @@
 def local(peers, groups, spectra_flux, pixel_weights, old_basis):
     spectra, pixels = pixel_weights.shape
     rank = old_basis.shape[0]
-    share, chunk = pixels // peers, spectra // groups
+    half, chunk = pixels // 2, spectra // groups
+    rows = up(chunk, ROWS)
     lead = pair_rows(rank)
     wide = up(lead + rank, LANES)
-    me = lax.axis_index("spec").astype(jnp.int32).reshape(1)
-
-    gram, *picks = call(
-        functools.partial(spec_kernel, peers=peers, chunk=chunk),
-        [shape(groups, up(chunk, ROWS), wide)] + [shape(2, spectra, share)] * peers,
-        [(2 * rank, pixels), (lead, pixels)],
-        me,
-        spectra_flux,
-        pixel_weights,
-        old_basis,
-        smem=1,
-    )
-
-    def swap(value, q):
-        return lax.ppermute(value, "spec", [(s, s ^ q) for s in range(peers)])
-
-    picks = [picks[0]] + [swap(picks[q], q) for q in range(1, peers)]
-    parts = lax.all_to_all(gram, "pix", 0, 0)
+    inputs = [pltpu.with_memory_space_constraint(a, pltpu.HBM) for a in (spectra_flux, pixel_weights, old_basis)]
+
+    def swap(value, axis, mask):
+        return lax.ppermute(value, axis, [(s, s ^ mask) for s in range(peers if axis == "spec" else groups)])
+
+    keep, send, own, other = call(
+        functools.partial(spec_kernel, chunk=chunk),
+        [shape(groups // 2, rows, wide)] * 2 + [shape(2, spectra, half)] * 2,
+        [
+            (spectra, pixels),
+            (spectra, pixels),
+            (rank, pixels),
+            (2 * rank, pixels),
+            (lead, pixels),
+            (groups, rows, wide),
+            pltpu.SemaphoreType.DMA((3,)),
+        ],
+        *inputs,
+        space=pl.ANY,
+    )
+    arrived = swap(send, "pix", 1)
+    picks = [own] + [swap(other if q & 1 else own, "spec", q) for q in range(1, peers)]
+    sums = call(fold_kernel, [shape(rows, wide)] * (groups // 2), [], keep, arrived)
+    parts = [sums[0]] + [swap(sums[k], "pix", 2 * k) for k in range(1, groups // 2)]
     tiles = call(
         functools.partial(coeff_kernel, rank=rank, chunk=chunk),
         shape(peers * groups, ROWS, LANES),
         [(wide, LANES), (rank * rank, LANES), (rank * rank, LANES)],
-        parts,
+        *parts,
     )
     tiles = lax.all_to_all(tiles, ("spec", "pix"), 0, 0)
     depth = peers * spectra
-    basis_share = call(
+    mine = call(
         functools.partial(pixel_kernel, peers=peers, rank=rank, chunk=chunk),
-        shape(rank, share),
+        shape(rank, half),
         [
             (2 * rank, up(depth, LANES)),
             (lead, up(depth, LANES)),
-            (2, depth, share),
-            (rank * rank, LANES),
-            (rank * rank, LANES),
+            (2, depth, half),
+            (half // LANES, rank * rank, LANES),
+            (half // LANES, rank * rank, LANES),
         ],
-        me,
         tiles,
         *picks,
-        smem=1,
-    )
-    shares = [basis_share] + [swap(basis_share, q) for q in range(1, peers)]
-    return call(functools.partial(place_kernel, peers=peers), shape(rank, pixels), [], me, *shares, smem=1)
+    )
+    return call(place_kernel, shape(rank, pixels), [], mine, swap(mine, "spec", 1))
 
 
 def solution(mesh):

time: 51.7 us -> 43.6 us (0.84)
  blocking collectives: 20.9 us -> 0 us
  starting transfers between devices: 7.7 us -> 18.6 us
  local copies, waits for them, and re-layouts: 2.83 us -> 0 us
  Pallas kernels: 6.4 us -> 9.04 us
  waiting for transfers between devices: 13.6 us -> 15.8 us
    all_to_all x1 -> x0, blocking collectives: 20.9 us -> none  [local(): parts = lax.all_to_all(gram, 'pix', 0, 0)]
    ppermute x6 -> x8, starting transfers between devices: 4.07 us -> 13.1 us  [swap(): lax.ppermute(value, axis, [(s, s ^ mask) for s in range(peers if axis ==...]
    all_to_all x1, waiting for transfers between devices: 0.01 us -> 7.71 us  [local(): tiles = lax.all_to_all(tiles, ('spec', 'pix'), 0, 0)]
    ppermute x6 -> x8, waiting for transfers between devices: 13.6 us -> 8.06 us  [swap(): lax.ppermute(value, axis, [(s, s ^ mask) for s in range(peers if axis ==...]
    unnamed x6 -> x0, local copies, waits for them, and re-layouts: 2.83 us -> none
    pallas_call x4 -> x5, Pallas kernels: 6.4 us -> 9.04 us  [call(): pl.pallas_call(kernel, out_shape=outs, in_specs=[pl.BlockSpec(memory_spac...]
    all_to_all x1, starting transfers between devices: 3.64 us -> 5.52 us  [local(): tiles = lax.all_to_all(tiles, ('spec', 'pix'), 0, 0)]
  transfers between devices with their start and end apart: 7 -> 9, of which waited for: 4 -> 6; matrix products, arithmetic and copies ran while one was open for 0% -> 0% of each run, Pallas kernels for 0% -> 3%
where the time goes in v1:
time: 43.6 us; the launch traced here: 43.4 us
  starting transfers between devices  18.6 us (43%)
  waiting for transfers between devices  15.8 us (36%)
  Pallas kernels  9.04 us (21%)
    ppermute x8, starting transfers between devices, swap(): lax.ppermute(value, axis, [(s, s ^ mask) for s in range(peers if axis ==...  13.1 us
    pallas_call x5, Pallas kernels, call(): pl.pallas_call(kernel, out_shape=outs, in_specs=[pl.BlockSpec(memory_spac...  9.04 us
    ppermute x8, waiting for transfers between devices, swap(): lax.ppermute(value, axis, [(s, s ^ mask) for s in range(peers if axis ==...  8.06 us
    all_to_all x1, waiting for transfers between devices, local(): tiles = lax.all_to_all(tiles, ('spec', 'pix'), 0, 0)  7.71 us
    all_to_all x1, starting transfers between devices, local(): tiles = lax.all_to_all(tiles, ('spec', 'pix'), 0, 0)  5.52 us
  transfers between devices with their start and end apart: 9, of which 6 were waited for; matrix products, arithmetic and copies ran while one was open for 0% of the time, Pallas kernels for 3%

profile of v1, /device:TPU:0, one launch (start us, length us, event | category | flops | bytes accessed | tf_op | source)
XLA Modules:
  0.0 43.4 jit_solution(7131460917169872368)
XLA Ops:
  0.0 3.7 %shard_map.37 = (f32[4,24,640]{2,1,0:T(8,128)S(1)}, f32[4,24,640]{2,1,0:T(8,128)S(1)}, f32[2,192,256]{2,1,0:T(8,128)S(1)}, f32[2,192,256]{2,1,0:T(8,128)S(1)}) custom-call(f32[192,512]{1,0:T(8,128)} %flux_hbm.1, f32[192,512]{1,0:T(8,128)} %weights_hbm.1, f32[32,512]{1,0:T(8,128)} %basis_hbm.1), custom_call_target="tpu_custom_call" | custom-call | tf_op jit(solution)/shard_map/pallas_call | solution.py:180
  3.7 3.0 %collective-permute-start = (f32[4,24,640]{2,1,0:T(8,128)S(1)}, f32[4,24,640]{2,1,0:T(8,128)S(1)}, u32[]{:S(2)}, u32[]{:S(2)}) collective-permute-start(f32[4,24,640]{2,1,0:T(8,128)S(1)} %get-tuple-element.14), channel_id=1, source_target_pairs={{0,1},{1,0},{2,3},{3,2},{4,5},{5,4},{6,7},{7,6},{8,9},{9,8},{10,11... | collective-permute-start | bytes 737288 | tf_op jit(solution)/shard_map/ppermute | solution.py:204
  6.7 1.5 %collective-permute-start.5 = (f32[2,192,256]{2,1,0:T(8,128)S(1)}, f32[2,192,256]{2,1,0:T(8,128)S(1)}, u32[]{:S(2)}, u32[]{:S(2)}) collective-permute-start(f32[2,192,256]{2,1,0:T(8,128)S(1)} %get-tuple-element.19.rest_0_), channel_id=1, source_target_pairs={{0,16},{8,24},{16,0},{24,8},{1,17},{9,25},{17,1},{25,9},{2,18},{10... | collective-permute-start | bytes 1179656 | tf_op jit(solution)/shard_map/ppermute | solution.py:204
  8.2 0.0 collective-permute-start.6
  8.2 0.6 %collective-permute-start.4 = (f32[2,192,256]{2,1,0:T(8,128)S(1)}, f32[2,192,256]{2,1,0:T(8,128)S(1)}, u32[]{:S(2)}, u32[]{:S(2)}) collective-permute-start(f32[2,192,256]{2,1,0:T(8,128)S(1)} %get-tuple-element.20), channel_id=1, source_target_pairs={{0,8},{8,0},{16,24},{24,16},{1,9},{9,1},{17,25},{25,17},{2,10},{10... | collective-permute-start | bytes 1179656 | tf_op jit(solution)/shard_map/ppermute | solution.py:204
  8.9 3.8 %collective-permute-done.arrived = f32[4,24,640]{2,1,0:T(8,128)S(1)} collective-permute-done((f32[4,24,640]{2,1,0:T(8,128)S(1)}, f32[4,24,640]{2,1,0:T(8,128)S(1)}, u32[]{:S(2)}, u32[]{:S(2)}) %collective-permute-start) | collective-permute-done | bytes 245792 | tf_op jit(solution)/shard_map/ppermute | solution.py:204
  12.7 1.9 %collective-permute-start.1 = (f32[24,640]{1,0:T(8,128)S(1)}, f32[24,640]{1,0:T(8,128)S(1)}, u32[]{:S(2)}, u32[]{:S(2)}) collective-permute-start(f32[24,640]{1,0:T(8,128)S(1)} %get-tuple-element.16), channel_id=1, source_target_pairs={{0,2},{1,3},{2,0},{3,1},{4,6},{5,7},{6,4},{7,5},{8,10},{9,11},{10,... | collective-permute-start | bytes 184328 | tf_op jit(solution)/shard_map/ppermute | solution.py:204
  14.6 2.6 %collective-permute-start.2 = (f32[24,640]{1,0:T(8,128)S(1)}, f32[24,640]{1,0:T(8,128)S(1)}, u32[]{:S(2)}, u32[]{:S(2)}) collective-permute-start(f32[24,640]{1,0:T(8,128)S(1)} %get-tuple-element.17), channel_id=1, source_target_pairs={{0,4},{1,5},{2,6},{3,7},{4,0},{5,1},{6,2},{7,3},{8,12},{9,13},{10,... | collective-permute-start | bytes 184328 | tf_op jit(solution)/shard_map/ppermute | solution.py:204
  17.2 0.4 collective-permute-done.1.refs_1_
  17.6 3.3 %collective-permute-start.3 = (f32[24,640]{1,0:T(8,128)S(1)}, f32[24,640]{1,0:T(8,128)S(1)}, u32[]{:S(2)}, u32[]{:S(2)}) collective-permute-start(f32[24,640]{1,0:T(8,128)S(1)} %get-tuple-element.18), channel_id=1, source_target_pairs={{0,6},{1,7},{2,4},{3,5},{4,2},{5,3},{6,0},{7,1},{8,14},{9,15},{10,... | collective-permute-start | bytes 184328 | tf_op jit(solution)/shard_map/ppermute | solution.py:204
  20.8 0.7 %collective-permute-done.2.refs_2_ = f32[24,640]{1,0:T(8,128)S(1)} collective-permute-done((f32[24,640]{1,0:T(8,128)S(1)}, f32[24,640]{1,0:T(8,128)S(1)}, u32[]{:S(2)}, u32[]{:S(2)}) %collective-permute-start.2) | collective-permute-done | bytes 61472 | tf_op jit(solution)/shard_map/ppermute | solution.py:204
  21.6 2.0 %collective-permute-done.3.refs_3_ = f32[24,640]{1,0:T(8,128)S(1)} collective-permute-done((f32[24,640]{1,0:T(8,128)S(1)}, f32[24,640]{1,0:T(8,128)S(1)}, u32[]{:S(2)}, u32[]{:S(2)}) %collective-permute-start.3) | collective-permute-done | bytes 61472 | tf_op jit(solution)/shard_map/ppermute | solution.py:204
  23.6 1.4 %shard_map.39 = f32[32,8,128]{2,1,0:T(8,128)} custom-call(f32[24,640]{1,0:T(8,128)S(1)} %get-tuple-element.15.refs_0_, f32[24,640]{1,0:T(8,128)S(1)} %collective-permute-done.1.refs_1_, f32[24,640]{1,0:T(8,128)S(1)} %collective-permute-done.2.refs_2_, f32[24,640]{1,0:T(8,128)S(1)} %collective-permute-done.3.refs_3_), custom_call_target="tpu_custom_call" | custom-call | tf_op jit(solution)/shard_map/pallas_call | solution.py:180
  25.0 5.5 %all-to-all-start = ((f32[32,8,128]{2,1,0:T(8,128)}), f32[32,8,128]{2,1,0:T(8,128)S(1)}, u32[]{:S(2)}, u32[]{:S(2)}) async-start(f32[32,8,128]{2,1,0:T(8,128)} %shard_map.39), calls=%async_computation | async-start | bytes 262144 | tf_op jit(solution)/shard_map/all_to_all | solution.py:231
  30.6 0.0 collective-permute-done.5.rest_2_
  30.6 0.0 collective-permute-done.6.rest_3_
  30.6 0.0 collective-permute-done.4.rest_1_
  30.6 7.7 %all-to-all-done.tiles = f32[32,8,128]{2,1,0:T(8,128)S(1)} async-done(((f32[32,8,128]{2,1,0:T(8,128)}), f32[32,8,128]{2,1,0:T(8,128)S(1)}, u32[]{:S(2)}, u32[]{:S(2)}) %all-to-all-start) | async-done | bytes 131104 | tf_op jit(solution)/shard_map/all_to_all | solution.py:231
  38.3 3.2 %shard_map.40.own = f32[32,256]{1,0:T(8,128)S(1)} custom-call(f32[32,8,128]{2,1,0:T(8,128)S(1)} %all-to-all-done.tiles, f32[2,192,256]{2,1,0:T(8,128)S(1)} %get-tuple-element.19.rest_0_, f32[2,192,256]{2,1,0:T(8,128)S(1)} %collective-permute-done.4.rest_1_, f32[2,192,256]{2,1,0:T(8,128)S(1)} %collective-permute-done.5.rest_2_, ...), custom_call_target="tpu_custom_call" | custom-call | tf_op jit(solution)/shard_map/pallas_call | solution.py:180
  41.5 0.2 collective-permute-start.7
  41.7 1.1 %collective-permute-done.7.other = f32[32,256]{1,0:T(8,128)S(1)} collective-permute-done((f32[32,256]{1,0:T(8,128)S(1)}, f32[32,256]{1,0:T(8,128)S(1)}, u32[]{:S(2)}, u32[]{:S(2)}) %collective-permute-start.7) | collective-permute-done | bytes 32800 | tf_op jit(solution)/shard_map/ppermute | solution.py:204
  42.8 0.6 %shard_map.41 = f32[32,512]{1,0:T(8,128)} custom-call(f32[32,256]{1,0:T(8,128)S(1)} %shard_map.40.own, f32[32,256]{1,0:T(8,128)S(1)} %collective-permute-done.7.other), custom_call_target="tpu_custom_call" | custom-call | tf_op jit(solution)/shard_map/pallas_call | solution.py:180
  (1 shorter events, 0.0 us)
Async XLA Ops:
  3.7 9.0 %collective-permute-start = (f32[4,24,640]{2,1,0:T(8,128)S(1)}, f32[4,24,640]{2,1,0:T(8,128)S(1)}, u32[]{:S(2)}, u32[]{:S(2)}) collective-permute-start(f32[4,24,640]{2,1,0:T(8,128)S(1)} %get-tuple-element.14), channel_id=1, source_target_pairs={{0,1},{1,0},{2,3},{3,2},{4,5},{5,4},{6,7},{7,6},{8,9},{9,8},{10,11... | collective-permute-start | bytes 737288 | tf_op jit(solution)/shard_map/ppermute | solution.py:204
  6.7 23.9 %collective-permute-start.5 = (f32[2,192,256]{2,1,0:T(8,128)S(1)}, f32[2,192,256]{2,1,0:T(8,128)S(1)}, u32[]{:S(2)}, u32[]{:S(2)}) collective-permute-start(f32[2,192,256]{2,1,0:T(8,128)S(1)} %get-tuple-element.19.rest_0_), channel_id=1, source_target_pairs={{0,16},{8,24},{16,0},{24,8},{1,17},{9,25},{17,1},{25,9},{2,18},{10... | collective-permute-start | bytes 1179656 | tf_op jit(solution)/shard_map/ppermute | solution.py:204
  8.2 22.3 %collective-permute-start.6 = (f32[2,192,256]{2,1,0:T(8,128)S(1)}, f32[2,192,256]{2,1,0:T(8,128)S(1)}, u32[]{:S(2)}, u32[]{:S(2)}) collective-permute-start(f32[2,192,256]{2,1,0:T(8,128)S(1)} %get-tuple-element.20), channel_id=1, source_target_pairs={{0,24},{8,16},{16,8},{24,0},{1,25},{9,17},{17,9},{25,1},{2,26},{10... | collective-permute-start | bytes 1179656 | tf_op jit(solution)/shard_map/ppermute | solution.py:204
  8.2 22.3 %collective-permute-start.4 = (f32[2,192,256]{2,1,0:T(8,128)S(1)}, f32[2,192,256]{2,1,0:T(8,128)S(1)}, u32[]{:S(2)}, u32[]{:S(2)}) collective-permute-start(f32[2,192,256]{2,1,0:T(8,128)S(1)} %get-tuple-element.20), channel_id=1, source_target_pairs={{0,8},{8,0},{16,24},{24,16},{1,9},{9,1},{17,25},{25,17},{2,10},{10... | collective-permute-start | bytes 1179656 | tf_op jit(solution)/shard_map/ppermute | solution.py:204
  12.7 4.9 %collective-permute-start.1 = (f32[24,640]{1,0:T(8,128)S(1)}, f32[24,640]{1,0:T(8,128)S(1)}, u32[]{:S(2)}, u32[]{:S(2)}) collective-permute-start(f32[24,640]{1,0:T(8,128)S(1)} %get-tuple-element.16), channel_id=1, source_target_pairs={{0,2},{1,3},{2,0},{3,1},{4,6},{5,7},{6,4},{7,5},{8,10},{9,11},{10,... | collective-permute-start | bytes 184328 | tf_op jit(solution)/shard_map/ppermute | solution.py:204
  14.6 7.0 %collective-permute-start.2 = (f32[24,640]{1,0:T(8,128)S(1)}, f32[24,640]{1,0:T(8,128)S(1)}, u32[]{:S(2)}, u32[]{:S(2)}) collective-permute-start(f32[24,640]{1,0:T(8,128)S(1)} %get-tuple-element.17), channel_id=1, source_target_pairs={{0,4},{1,5},{2,6},{3,7},{4,0},{5,1},{6,2},{7,3},{8,12},{9,13},{10,... | collective-permute-start | bytes 184328 | tf_op jit(solution)/shard_map/ppermute | solution.py:204
  17.6 6.0 %collective-permute-start.3 = (f32[24,640]{1,0:T(8,128)S(1)}, f32[24,640]{1,0:T(8,128)S(1)}, u32[]{:S(2)}, u32[]{:S(2)}) collective-permute-start(f32[24,640]{1,0:T(8,128)S(1)} %get-tuple-element.18), channel_id=1, source_target_pairs={{0,6},{1,7},{2,4},{3,5},{4,2},{5,3},{6,0},{7,1},{8,14},{9,15},{10,... | collective-permute-start | bytes 184328 | tf_op jit(solution)/shard_map/ppermute | solution.py:204
  25.0 13.3 %all-to-all-start = ((f32[32,8,128]{2,1,0:T(8,128)}), f32[32,8,128]{2,1,0:T(8,128)S(1)}, u32[]{:S(2)}, u32[]{:S(2)}) async-start(f32[32,8,128]{2,1,0:T(8,128)} %shard_map.39), calls=%async_computation | async-start | bytes 262144 | tf_op jit(solution)/shard_map/all_to_all | solution.py:231
  41.5 1.3 %collective-permute-start.7 = (f32[32,256]{1,0:T(8,128)S(1)}, f32[32,256]{1,0:T(8,128)S(1)}, u32[]{:S(2)}, u32[]{:S(2)}) collective-permute-start(f32[32,256]{1,0:T(8,128)S(1)} %shard_map.40.own), channel_id=1, source_target_pairs={{0,8},{8,0},{16,24},{24,16},{1,9},{9,1},{17,25},{25,17},{2,10},{10... | collective-permute-start | bytes 98312 | tf_op jit(solution)/shard_map/ppermute | solution.py:204

commit v2 on v1

v2 whole, which is shorter than its diff:
```python
import functools

import jax
import jax.numpy as jnp
from jax import lax
from jax.experimental import pallas as pl
from jax.experimental.pallas import tpu as pltpu
from jax.sharding import PartitionSpec as P

LANES = 128
ROWS = 8
VMEM = pl.BlockSpec(memory_space=pltpu.VMEM)
LIMIT = 48 * 1024 * 1024


def up(value, multiple):
    return -(-value // multiple) * multiple


def pair_rows(rank):
    return rank * (rank // 2) + rank // 2


def halves(value):
    high = value.astype(jnp.bfloat16)
    return high, (value - high.astype(jnp.float32)).astype(jnp.bfloat16)


def write_pairs(twice, high, low, rank):
    first = twice[0:rank, :]
    for diag in range(rank // 2 + 1):
        count = rank if diag < rank // 2 else rank // 2
        rows = slice(diag * rank, diag * rank + count)
        high[rows, :], low[rows, :] = halves(first[0:count] * twice[diag : diag + count, :])


def unpack(packed, full, rank):
    for diag in range(rank // 2 + 1):
        base = diag * rank
        count = rank if diag < rank // 2 else rank // 2
        wrap = min(count, rank - diag)
        part = packed[base : base + wrap, :]
        full[pl.ds(diag, wrap, stride=rank + 1), :] = part
        if diag:
            full[pl.ds(diag * rank, wrap, stride=rank + 1), :] = part
        if wrap < count:
            part = packed[base + wrap : base + count, :]
            full[pl.ds(rank - diag, count - wrap, stride=rank + 1), :] = part
            full[pl.ds((rank - diag) * rank, count - wrap, stride=rank + 1), :] = part


def solve(fulls, targets, scaleds, rank):
    row = lax.broadcasted_iota(jnp.int32, targets[0].shape, 0)
    targets, pivots = list(targets), [jnp.zeros_like(target) for target in targets]
    for k in range(rank):
        here = row == k
        for t, (full, scaled) in enumerate(zip(fulls, scaleds)):
            column = full[k * rank : (k + 1) * rank, :]
            for j in range(k):
                column = column - scaled[j * rank : (j + 1) * rank, :] * full[j * rank + k : j * rank + k + 1, :]
            full[k * rank : (k + 1) * rank, :] = column
            factor = jnp.where(here, 0.0, column * (1.0 / column[k : k + 1, :]))
            scaled[k * rank : (k + 1) * rank, :] = factor
            pivots[t] = jnp.where(here, column, pivots[t])
            targets[t] = targets[t] - factor * targets[t][k : k + 1, :]
    return [target / pivot for target, pivot in zip(targets, pivots)]


def dot(left, right, right_axis):
    return lax.dot_general(
        left, right, (((1,), (right_axis,)), ((), ())), preferred_element_type=jnp.float32
    )


def layout(rank, chunk):
    rows = up(chunk, ROWS)
    whole, rest = divmod(pair_rows(rank) + rank, LANES)
    beside = LANES // rest if rest else 1
    tail = -(-(rows // ROWS) // beside) if rest else 0
    return rows, whole, rest, beside, rows * whole + ROWS * tail


def spec_kernel(flux_hbm, weights_hbm, basis_hbm, keep, send, own, other, *scratch, chunk):
    flux, weights, basis, twice, high, low, both, terms, last, grams, sems = scratch
    copies = [
        pltpu.make_async_copy(source, target, sems.at[k])
        for k, (source, target) in enumerate(((basis_hbm, basis), (weights_hbm, weights), (flux_hbm, flux)))
    ]
    for copy in copies:
        copy.start()
    rank, pixels = basis.shape
    spectra = weights.shape[0]
    half = own.shape[2]
    lead = pair_rows(rank)
    copies[0].wait()
    twice[0:rank, :] = basis[...]
    twice[rank:, :] = basis[...]
    terms[0:rank, :], terms[rank:, :] = halves(basis[...])
    write_pairs(twice, high, low, rank)
    copies[1].wait()
    both[0:spectra, :], both[spectra:, :] = halves(weights[...])
    part = dot(both[...], high[...], 1)
    packed = part[spectra:] + dot(both[0:spectra, :], low[...], 1) + part[0:spectra]
    copies[2].wait()
    flux[...] = weights[...] * flux[...]
    both[0:spectra, :], both[spectra:, :] = halves(flux[...])
    part = dot(both[...], terms[...], 1)
    target = part[spectra:, 0:rank] + part[0:spectra, rank:] + part[0:spectra, 0:rank]
    rows, whole, rest, beside, _ = layout(rank, chunk)
    last[:, 0 : rest - rank] = packed[:, lead + rank - rest :]
    last[:, rest - rank : rest] = target
    for k in range(grams.shape[0]):
        for t in range(whole):
            grams[k, t * rows : t * rows + chunk, :] = packed[k * chunk : (k + 1) * chunk, t * LANES : (t + 1) * LANES]
        for g in range(rows // ROWS):
            base, count = rows * whole + g // beside * ROWS, min(ROWS, chunk - g * ROWS)
            lanes = slice(g % beside * rest, (g % beside + 1) * rest)
            grams[k, base : base + count, lanes] = last[k * chunk + g * ROWS : k * chunk + g * ROWS + count, 0:rest]
    for k in range(grams.shape[0] // 2):
        keep[k] = grams[lax.axis_index("pix") ^ (2 * k)]
        send[k] = grams[lax.axis_index("pix") ^ (2 * k + 1)]
    near = pl.multiple_of((lax.axis_index("spec") & 1) * half, LANES)
    far = pl.multiple_of(half - near, LANES)
    own[0] = weights[:, pl.ds(near, half)]
    own[1] = flux[:, pl.ds(near, half)]
    other[0] = weights[:, pl.ds(far, half)]
    other[1] = flux[:, pl.ds(far, half)]


def fold_kernel(keep, arrived, *outs):
    for k, out in enumerate(outs):
        out[...] = keep[k] + arrived[k]


def coeff_kernel(*refs, rank, chunk):
    parts, (out, packed, full, scaled) = refs[:-4], refs[-4:]
    total = parts[0][...]
    for part in parts[1:]:
        total = total + part[...]
    rows, whole, rest, beside, _ = layout(rank, chunk)
    filler = jnp.ones((LANES - rows, LANES), jnp.float32)
    blocks = [total[k * rows : (k + 1) * rows] for k in range(whole)]
    groups = []
    for g in range(rows // ROWS):
        base = rows * whole + g // beside * ROWS
        group = total[base : base + ROWS]
        groups.append(pltpu.roll(group, LANES - g % beside * rest, 1) if g % beside else group)
    blocks.append(jnp.concatenate(groups, axis=0))
    for k, block in enumerate(blocks):
        packed[k * LANES : (k + 1) * LANES, :] = jnp.concatenate([block, filler], axis=0).T
    lead = pair_rows(rank)
    unpack(packed, full, rank)
    (solved,) = solve([full], [packed[lead : lead + rank, :]], [scaled], rank)
    lane = lax.broadcasted_iota(jnp.int32, (ROWS, LANES), 1)
    tile = jnp.zeros((ROWS, LANES), jnp.float32)
    for a in range(rank // ROWS):
        part = solved[a * ROWS : (a + 1) * ROWS, :]
        if a:
            part = pltpu.roll(part, a * chunk, 1)
        tile = jnp.where((lane >= a * chunk) & (lane < (a + 1) * chunk), part, tile)
    for k in range(out.shape[0]):
        out[k] = tile


def pixel_kernel(tiles, *rest, peers, rank, chunk):
    picks, (out, twice, pairs, high, low, full, scaled) = rest[:peers], rest[peers:]
    spectra = picks[0].shape[1]
    half = picks[0].shape[2]
    group = spectra // chunk
    lane = lax.broadcasted_iota(jnp.int32, (ROWS, LANES), 1)
    width = twice.shape[1]
    for q in range(peers):
        rows = slice(q * spectra, (q + 1) * spectra)
        for k in range(2):
            high[k, rows, :], low[k, rows, :] = halves(picks[q][k])
    for a in range(rank // ROWS):
        columns = [jnp.zeros((ROWS, LANES), jnp.float32) for _ in range(width // LANES)]
        for q in range(peers):
            for k in range(group):
                part = tiles[(lax.axis_index("spec") ^ q) * group + k]
                start = q * spectra + k * chunk
                shift = (start - a * chunk) % LANES
                if shift:
                    part = pltpu.roll(part, shift, 1)
                for t in range(start // LANES, (start + chunk - 1) // LANES + 1):
                    begin, end = max(start - t * LANES, 0), min(start + chunk - t * LANES, LANES)
                    columns[t] = jnp.where((lane >= begin) & (lane < end), part, columns[t])
        for t, column in enumerate(columns):
            twice[a * ROWS : (a + 1) * ROWS, t * LANES : (t + 1) * LANES] = column
            twice[rank + a * ROWS : rank + (a + 1) * ROWS, t * LANES : (t + 1) * LANES] = column
    depth = high.shape[1]
    lead = pair_rows(rank)
    write_pairs(twice, pairs.at[0:lead], pairs.at[lead : 2 * lead], rank)
    part = dot(pairs[:, 0:depth], high[0], 0)
    packed = part[lead:] + dot(pairs[0:lead, 0:depth], low[0], 0) + part[0:lead]
    terms = jnp.concatenate(halves(twice[0:rank, 0:depth]), axis=0)
    part = dot(terms, high[1], 0)
    target = part[rank:] + dot(terms[0:rank], low[1], 0) + part[0:rank]
    tiles = range(half // LANES)
    for t in tiles:
        unpack(packed[:, t * LANES : (t + 1) * LANES], full.at[t], rank)
    solved = solve(
        [full.at[t] for t in tiles],
        [target[:, t * LANES : (t + 1) * LANES] for t in tiles],
        [scaled.at[t] for t in tiles],
        rank,
    )
    for t in tiles:
        out[:, t * LANES : (t + 1) * LANES] = solved[t]


def place_kernel(own, other, out):
    half = own.shape[1]
    low = pl.multiple_of((lax.axis_index("spec") & 1) * half, LANES)
    out[:, pl.ds(low, half)] = own[...]
    out[:, pl.ds(pl.multiple_of(half - low, LANES), half)] = other[...]


def scratch_shape(sizes):
    if not isinstance(sizes, tuple):
        return sizes
    if sizes[0] is jnp.bfloat16:
        return pltpu.VMEM(sizes[1:], jnp.bfloat16)
    return pltpu.VMEM(sizes, jnp.float32)


def call(kernel, outs, scratch, *args, space=pltpu.VMEM):
    return pl.pallas_call(
        kernel,
        out_shape=outs,
        in_specs=[pl.BlockSpec(memory_space=space)] * len(args),
        out_specs=jax.tree.map(lambda _: VMEM, outs),
        scratch_shapes=[scratch_shape(s) for s in scratch],
        compiler_params=pltpu.CompilerParams(vmem_limit_bytes=LIMIT),
    )(*args)


def shape(*sizes):
    return jax.ShapeDtypeStruct(sizes, jnp.float32)


def local(peers, groups, spectra_flux, pixel_weights, old_basis):
    spectra, pixels = pixel_weights.shape
    rank = old_basis.shape[0]
    half, chunk = pixels // 2, spectra // groups
    lead = pair_rows(rank)
    wide = up(lead + rank, LANES)
    rows = layout(rank, chunk)[-1]
    half_type = jnp.bfloat16
    inputs = [pltpu.with_memory_space_constraint(a, pltpu.HBM) for a in (spectra_flux, pixel_weights, old_basis)]

    def swap(value, axis, mask):
        return lax.ppermute(value, axis, [(s, s ^ mask) for s in range(peers if axis == "spec" else groups)])

    keep, send, own, other = call(
        functools.partial(spec_kernel, chunk=chunk),
        [shape(groups // 2, rows, LANES)] * 2 + [shape(2, spectra, half)] * 2,
        [
            (spectra, pixels),
            (spectra, pixels),
            (rank, pixels),
            (2 * rank, pixels),
            (half_type, lead, pixels),
            (half_type, lead, pixels),
            (half_type, 2 * spectra, pixels),
            (half_type, 2 * rank, pixels),
            (spectra, LANES),
            (groups, rows, LANES),
            pltpu.SemaphoreType.DMA((3,)),
        ],
        *inputs,
        space=pl.ANY,
    )
    arrived = swap(send, "pix", 1)
    picks = [own] + [swap(other if q & 1 else own, "spec", q) for q in range(1, peers)]
    sums = call(fold_kernel, [shape(rows, LANES)] * (groups // 2), [], keep, arrived)
    parts = [sums[0]] + [swap(sums[k], "pix", 2 * k) for k in range(1, groups // 2)]
    tiles = call(
        functools.partial(coeff_kernel, rank=rank, chunk=chunk),
        shape(peers * groups, ROWS, LANES),
        [(wide, LANES), (rank * rank, LANES), (rank * rank, LANES)],
        *parts,
    )
    tiles = lax.all_to_all(tiles, ("spec", "pix"), 0, 0)
    depth = peers * spectra
    mine = call(
        functools.partial(pixel_kernel, peers=peers, rank=rank, chunk=chunk),
        shape(rank, half),
        [
            (2 * rank, up(depth, LANES)),
            (half_type, 2 * lead, up(depth, LANES)),
            (half_type, 2, depth, half),
            (half_type, 2, depth, half),
            (half // LANES, rank * rank, LANES),
            (half // LANES, rank * rank, LANES),
        ],
        tiles,
        *picks,
    )
    return call(place_kernel, shape(rank, pixels), [], mine, swap(mine, "spec", 1))


def solution(mesh):
    placed = (P("spec", "pix"), P("spec", "pix"), P(None, "pix"))
    body = functools.partial(local, mesh.shape["spec"], mesh.shape["pix"])
    return jax.shard_map(body, mesh=mesh, in_specs=placed, out_specs=P(None, "pix"), check_vma=False)
```

time: 43.6 us -> 41.1 us (0.943)
  Pallas kernels: 9.04 us -> 6.93 us
  waiting for transfers between devices: 15.8 us -> 15.2 us
    pallas_call x5, Pallas kernels: 9.04 us -> 6.93 us  [call(): pl.pallas_call(kernel, out_shape=outs, in_specs=[pl.BlockSpec(memory_spac...]
    ppermute x8, waiting for transfers between devices: 8.06 us -> 7.49 us  [swap(): lax.ppermute(value, axis, [(s, s ^ mask) for s in range(peers if axis ==...]
  transfers between devices with their start and end apart: 9 -> 9, of which waited for: 6 -> 6; matrix products, arithmetic and copies ran while one was open for 0% -> 0% of each run, Pallas kernels for 3% -> 4%
where the time goes in v2:
time: 41.1 us; the launch traced here: 40.9 us
  starting transfers between devices  18.7 us (45%)
  waiting for transfers between devices  15.2 us (37%)
  Pallas kernels  6.93 us (17%)
    ppermute x8, starting transfers between devices, swap(): lax.ppermute(value, axis, [(s, s ^ mask) for s in range(peers if axis ==...  13.1 us
    all_to_all x1, waiting for transfers between devices, local(): tiles = lax.all_to_all(tiles, ('spec', 'pix'), 0, 0)  7.71 us
    ppermute x8, waiting for transfers between devices, swap(): lax.ppermute(value, axis, [(s, s ^ mask) for s in range(peers if axis ==...  7.49 us
    pallas_call x5, Pallas kernels, call(): pl.pallas_call(kernel, out_shape=outs, in_specs=[pl.BlockSpec(memory_spac...  6.93 us
    all_to_all x1, starting transfers between devices, local(): tiles = lax.all_to_all(tiles, ('spec', 'pix'), 0, 0)  5.56 us
  transfers between devices with their start and end apart: 9, of which 6 were waited for; matrix products, arithmetic and copies ran while one was open for 0% of the time, Pallas kernels for 4%

profile of v2, /device:TPU:0, one launch (start us, length us, event | category | flops | bytes accessed | tf_op | source)
XLA Modules:
  0.0 40.9 jit_solution(9035795905120698148)
XLA Ops:
  0.0 2.5 %shard_map.37 = (f32[4,112,128]{2,1,0:T(8,128)S(1)}, f32[4,112,128]{2,1,0:T(8,128)S(1)}, f32[2,192,256]{2,1,0:T(8,128)S(1)}, f32[2,192,256]{2,1,0:T(8,128)S(1)}) custom-call(f32[192,512]{1,0:T(8,128)} %flux_hbm.1, f32[192,512]{1,0:T(8,128)} %weights_hbm.1, f32[32,512]{1,0:T(8,128)} %basis_hbm.1), custom_call_target="tpu_custom_call" | custom-call | tf_op jit(solution)/shard_map/pallas_call | solution.py:228
  2.5 3.0 %collective-permute-start = (f32[4,112,128]{2,1,0:T(8,128)S(1)}, f32[4,112,128]{2,1,0:T(8,128)S(1)}, u32[]{:S(2)}, u32[]{:S(2)}) collective-permute-start(f32[4,112,128]{2,1,0:T(8,128)S(1)} %get-tuple-element.14), channel_id=1, source_target_pairs={{0,1},{1,0},{2,3},{3,2},{4,5},{5,4},{6,7},{7,6},{8,9},{9,8},{10,11... | collective-permute-start | bytes 688136 | tf_op jit(solution)/shard_map/ppermute | solution.py:253
  5.5 1.5 %collective-permute-start.5 = (f32[2,192,256]{2,1,0:T(8,128)S(1)}, f32[2,192,256]{2,1,0:T(8,128)S(1)}, u32[]{:S(2)}, u32[]{:S(2)}) collective-permute-start(f32[2,192,256]{2,1,0:T(8,128)S(1)} %get-tuple-element.19.rest_0_), channel_id=1, source_target_pairs={{0,16},{8,24},{16,0},{24,8},{1,17},{9,25},{17,1},{25,9},{2,18},{10... | collective-permute-start | bytes 1179656 | tf_op jit(solution)/shard_map/ppermute | solution.py:253
  7.0 0.0 collective-permute-start.6
  7.0 0.6 %collective-permute-start.4 = (f32[2,192,256]{2,1,0:T(8,128)S(1)}, f32[2,192,256]{2,1,0:T(8,128)S(1)}, u32[]{:S(2)}, u32[]{:S(2)}) collective-permute-start(f32[2,192,256]{2,1,0:T(8,128)S(1)} %get-tuple-element.20), channel_id=1, source_target_pairs={{0,8},{8,0},{16,24},{24,16},{1,9},{9,1},{17,25},{25,17},{2,10},{10... | collective-permute-start | bytes 1179656 | tf_op jit(solution)/shard_map/ppermute | solution.py:253
  7.6 3.4 %collective-permute-done.arrived = f32[4,112,128]{2,1,0:T(8,128)S(1)} collective-permute-done((f32[4,112,128]{2,1,0:T(8,128)S(1)}, f32[4,112,128]{2,1,0:T(8,128)S(1)}, u32[]{:S(2)}, u32[]{:S(2)}) %collective-permute-start) | collective-permute-done | bytes 229408 | tf_op jit(solution)/shard_map/ppermute | solution.py:253
  11.1 1.9 %collective-permute-start.1 = (f32[112,128]{1,0:T(8,128)S(1)}, f32[112,128]{1,0:T(8,128)S(1)}, u32[]{:S(2)}, u32[]{:S(2)}) collective-permute-start(f32[112,128]{1,0:T(8,128)S(1)} %get-tuple-element.16), channel_id=1, source_target_pairs={{0,2},{1,3},{2,0},{3,1},{4,6},{5,7},{6,4},{7,5},{8,10},{9,11},{10,... | collective-permute-start | bytes 172040 | tf_op jit(solution)/shard_map/ppermute | solution.py:253
  13.0 2.6 %collective-permute-start.2 = (f32[112,128]{1,0:T(8,128)S(1)}, f32[112,128]{1,0:T(8,128)S(1)}, u32[]{:S(2)}, u32[]{:S(2)}) collective-permute-start(f32[112,128]{1,0:T(8,128)S(1)} %get-tuple-element.17), channel_id=1, source_target_pairs={{0,4},{1,5},{2,6},{3,7},{4,0},{5,1},{6,2},{7,3},{8,12},{9,13},{10,... | collective-permute-start | bytes 172040 | tf_op jit(solution)/shard_map/ppermute | solution.py:253
  15.6 0.3 collective-permute-done.1.refs_1_
  15.9 3.3 %collective-permute-start.3 = (f32[112,128]{1,0:T(8,128)S(1)}, f32[112,128]{1,0:T(8,128)S(1)}, u32[]{:S(2)}, u32[]{:S(2)}) collective-permute-start(f32[112,128]{1,0:T(8,128)S(1)} %get-tuple-element.18), channel_id=1, source_target_pairs={{0,6},{1,7},{2,4},{3,5},{4,2},{5,3},{6,0},{7,1},{8,14},{9,15},{10,... | collective-permute-start | bytes 172040 | tf_op jit(solution)/shard_map/ppermute | solution.py:253
  19.2 0.6 %collective-permute-done.2.refs_2_ = f32[112,128]{1,0:T(8,128)S(1)} collective-permute-done((f32[112,128]{1,0:T(8,128)S(1)}, f32[112,128]{1,0:T(8,128)S(1)}, u32[]{:S(2)}, u32[]{:S(2)}) %collective-permute-start.2) | collective-permute-done | bytes 57376 | tf_op jit(solution)/shard_map/ppermute | solution.py:253
  19.8 2.1 %collective-permute-done.3.refs_3_ = f32[112,128]{1,0:T(8,128)S(1)} collective-permute-done((f32[112,128]{1,0:T(8,128)S(1)}, f32[112,128]{1,0:T(8,128)S(1)}, u32[]{:S(2)}, u32[]{:S(2)}) %collective-permute-start.3) | collective-permute-done | bytes 57376 | tf_op jit(solution)/shard_map/ppermute | solution.py:253
  21.9 1.5 %shard_map.39 = f32[32,8,128]{2,1,0:T(8,128)} custom-call(f32[112,128]{1,0:T(8,128)S(1)} %get-tuple-element.15.refs_0_, f32[112,128]{1,0:T(8,128)S(1)} %collective-permute-done.1.refs_1_, f32[112,128]{1,0:T(8,128)S(1)} %collective-permute-done.2.refs_2_, f32[112,128]{1,0:T(8,128)S(1)} %collective-permute-done.3.refs_3_), custom_call_target="tpu_custom_call" | custom-call | tf_op jit(solution)/shard_map/pallas_call | solution.py:228
  23.3 5.6 %all-to-all-start = ((f32[32,8,128]{2,1,0:T(8,128)}), f32[32,8,128]{2,1,0:T(8,128)S(1)}, u32[]{:S(2)}, u32[]{:S(2)}) async-start(f32[32,8,128]{2,1,0:T(8,128)} %shard_map.39), calls=%async_computation | async-start | bytes 262144 | tf_op jit(solution)/shard_map/all_to_all | solution.py:284
  28.9 0.0 collective-permute-done.5.rest_2_
  28.9 0.0 collective-permute-done.6.rest_3_
  28.9 0.0 collective-permute-done.4.rest_1_
  28.9 7.7 %all-to-all-done.tiles = f32[32,8,128]{2,1,0:T(8,128)S(1)} async-done(((f32[32,8,128]{2,1,0:T(8,128)}), f32[32,8,128]{2,1,0:T(8,128)S(1)}, u32[]{:S(2)}, u32[]{:S(2)}) %all-to-all-start) | async-done | bytes 131104 | tf_op jit(solution)/shard_map/all_to_all | solution.py:284
  36.6 2.3 %shard_map.40.own = f32[32,256]{1,0:T(8,128)S(1)} custom-call(f32[32,8,128]{2,1,0:T(8,128)S(1)} %all-to-all-done.tiles, f32[2,192,256]{2,1,0:T(8,128)S(1)} %get-tuple-element.19.rest_0_, f32[2,192,256]{2,1,0:T(8,128)S(1)} %collective-permute-done.4.rest_1_, f32[2,192,256]{2,1,0:T(8,128)S(1)} %collective-permute-done.5.rest_2_, ...), custom_call_target="tpu_custom_call" | custom-call | tf_op jit(solution)/shard_map/pallas_call | solution.py:228
  39.0 0.2 collective-permute-start.7
  39.2 1.1 %collective-permute-done.7.other = f32[32,256]{1,0:T(8,128)S(1)} collective-permute-done((f32[32,256]{1,0:T(8,128)S(1)}, f32[32,256]{1,0:T(8,128)S(1)}, u32[]{:S(2)}, u32[]{:S(2)}) %collective-permute-start.7) | collective-permute-done | bytes 32800 | tf_op jit(solution)/shard_map/ppermute | solution.py:253
  40.2 0.6 %shard_map.41 = f32[32,512]{1,0:T(8,128)} custom-call(f32[32,256]{1,0:T(8,128)S(1)} %shard_map.40.own, f32[32,256]{1,0:T(8,128)S(1)} %collective-permute-done.7.other), custom_call_target="tpu_custom_call" | custom-call | tf_op jit(solution)/shard_map/pallas_call | solution.py:228
  (1 shorter events, 0.0 us)
Async XLA Ops:
  2.5 8.6 %collective-permute-start = (f32[4,112,128]{2,1,0:T(8,128)S(1)}, f32[4,112,128]{2,1,0:T(8,128)S(1)}, u32[]{:S(2)}, u32[]{:S(2)}) collective-permute-start(f32[4,112,128]{2,1,0:T(8,128)S(1)} %get-tuple-element.14), channel_id=1, source_target_pairs={{0,1},{1,0},{2,3},{3,2},{4,5},{5,4},{6,7},{7,6},{8,9},{9,8},{10,11... | collective-permute-start | bytes 688136 | tf_op jit(solution)/shard_map/ppermute | solution.py:253
  5.5 23.4 %collective-permute-start.5 = (f32[2,192,256]{2,1,0:T(8,128)S(1)}, f32[2,192,256]{2,1,0:T(8,128)S(1)}, u32[]{:S(2)}, u32[]{:S(2)}) collective-permute-start(f32[2,192,256]{2,1,0:T(8,128)S(1)} %get-tuple-element.19.rest_0_), channel_id=1, source_target_pairs={{0,16},{8,24},{16,0},{24,8},{1,17},{9,25},{17,1},{25,9},{2,18},{10... | collective-permute-start | bytes 1179656 | tf_op jit(solution)/shard_map/ppermute | solution.py:253
  7.0 21.9 %collective-permute-start.6 = (f32[2,192,256]{2,1,0:T(8,128)S(1)}, f32[2,192,256]{2,1,0:T(8,128)S(1)}, u32[]{:S(2)}, u32[]{:S(2)}) collective-permute-start(f32[2,192,256]{2,1,0:T(8,128)S(1)} %get-tuple-element.20), channel_id=1, source_target_pairs={{0,24},{8,16},{16,8},{24,0},{1,25},{9,17},{17,9},{25,1},{2,26},{10... | collective-permute-start | bytes 1179656 | tf_op jit(solution)/shard_map/ppermute | solution.py:253
  7.0 21.9 %collective-permute-start.4 = (f32[2,192,256]{2,1,0:T(8,128)S(1)}, f32[2,192,256]{2,1,0:T(8,128)S(1)}, u32[]{:S(2)}, u32[]{:S(2)}) collective-permute-start(f32[2,192,256]{2,1,0:T(8,128)S(1)} %get-tuple-element.20), channel_id=1, source_target_pairs={{0,8},{8,0},{16,24},{24,16},{1,9},{9,1},{17,25},{25,17},{2,10},{10... | collective-permute-start | bytes 1179656 | tf_op jit(solution)/shard_map/ppermute | solution.py:253
  11.1 4.8 %collective-permute-start.1 = (f32[112,128]{1,0:T(8,128)S(1)}, f32[112,128]{1,0:T(8,128)S(1)}, u32[]{:S(2)}, u32[]{:S(2)}) collective-permute-start(f32[112,128]{1,0:T(8,128)S(1)} %get-tuple-element.16), channel_id=1, source_target_pairs={{0,2},{1,3},{2,0},{3,1},{4,6},{5,7},{6,4},{7,5},{8,10},{9,11},{10,... | collective-permute-start | bytes 172040 | tf_op jit(solution)/shard_map/ppermute | solution.py:253
  13.0 6.8 %collective-permute-start.2 = (f32[112,128]{1,0:T(8,128)S(1)}, f32[112,128]{1,0:T(8,128)S(1)}, u32[]{:S(2)}, u32[]{:S(2)}) collective-permute-start(f32[112,128]{1,0:T(8,128)S(1)} %get-tuple-element.17), channel_id=1, source_target_pairs={{0,4},{1,5},{2,6},{3,7},{4,0},{5,1},{6,2},{7,3},{8,12},{9,13},{10,... | collective-permute-start | bytes 172040 | tf_op jit(solution)/shard_map/ppermute | solution.py:253
  15.9 6.0 %collective-permute-start.3 = (f32[112,128]{1,0:T(8,128)S(1)}, f32[112,128]{1,0:T(8,128)S(1)}, u32[]{:S(2)}, u32[]{:S(2)}) collective-permute-start(f32[112,128]{1,0:T(8,128)S(1)} %get-tuple-element.18), channel_id=1, source_target_pairs={{0,6},{1,7},{2,4},{3,5},{4,2},{5,3},{6,0},{7,1},{8,14},{9,15},{10,... | collective-permute-start | bytes 172040 | tf_op jit(solution)/shard_map/ppermute | solution.py:253
  23.3 13.3 %all-to-all-start = ((f32[32,8,128]{2,1,0:T(8,128)}), f32[32,8,128]{2,1,0:T(8,128)S(1)}, u32[]{:S(2)}, u32[]{:S(2)}) async-start(f32[32,8,128]{2,1,0:T(8,128)} %shard_map.39), calls=%async_computation | async-start | bytes 262144 | tf_op jit(solution)/shard_map/all_to_all | solution.py:284
  39.0 1.3 %collective-permute-start.7 = (f32[32,256]{1,0:T(8,128)S(1)}, f32[32,256]{1,0:T(8,128)S(1)}, u32[]{:S(2)}, u32[]{:S(2)}) collective-permute-start(f32[32,256]{1,0:T(8,128)S(1)} %shard_map.40.own), channel_id=1, source_target_pairs={{0,8},{8,0},{16,24},{24,16},{1,9},{9,1},{17,25},{25,17},{2,10},{10... | collective-permute-start | bytes 98312 | tf_op jit(solution)/shard_map/ppermute | solution.py:253

commit v3 on v2

--- a/solution.py
+++ b/solution.py
@@ -10,7 +10,12 @@
 LANES = 128
 ROWS = 8
 VMEM = pl.BlockSpec(memory_space=pltpu.VMEM)
+SPAN = 4
 LIMIT = 48 * 1024 * 1024
+
+
+def pixel_place():
+    return lax.axis_index("high") * SPAN + lax.axis_index("low")
 
 
 def up(value, multiple):
@@ -80,17 +85,20 @@
     return rows, whole, rest, beside, rows * whole + ROWS * tail
 
 
-def spec_kernel(flux_hbm, weights_hbm, basis_hbm, keep, send, own, other, *scratch, chunk):
+def spec_kernel(flux_hbm, weights_hbm, basis_hbm, own, other, *rest, chunk, span):
+    sends, scratch = rest[:span], rest[span:]
     flux, weights, basis, twice, high, low, both, terms, last, grams, sems = scratch
-    copies = [
-        pltpu.make_async_copy(source, target, sems.at[k])
-        for k, (source, target) in enumerate(((basis_hbm, basis), (weights_hbm, weights), (flux_hbm, flux)))
-    ]
-    for copy in copies:
-        copy.start()
     rank, pixels = basis.shape
     spectra = weights.shape[0]
     half = own.shape[2]
+    near = pl.multiple_of((lax.axis_index("spec") & 1) * half, LANES)
+    far = pl.multiple_of(half - near, LANES)
+    moves = [(basis_hbm, basis), (weights_hbm, weights), (flux_hbm, flux)]
+    moves += [(flux_hbm.at[:, pl.ds(far, half)], other.at[1]), (weights_hbm.at[:, pl.ds(far, half)], other.at[0])]
+    moves += [(flux_hbm.at[:, pl.ds(near, half)], own.at[1]), (weights_hbm.at[:, pl.ds(near, half)], own.at[0])]
+    copies = [pltpu.make_async_copy(source, target, sems.at[k]) for k, (source, target) in enumerate(moves)]
+    for copy in copies:
+        copy.start()
     lead = pair_rows(rank)
     copies[0].wait()
     twice[0:rank, :] = basis[...]
@@ -116,68 +124,73 @@
             base, count = rows * whole + g // beside * ROWS, min(ROWS, chunk - g * ROWS)
             lanes = slice(g % beside * rest, (g % beside + 1) * rest)
             grams[k, base : base + count, lanes] = last[k * chunk + g * ROWS : k * chunk + g * ROWS + count, 0:rest]
-    for k in range(grams.shape[0] // 2):
-        keep[k] = grams[lax.axis_index("pix") ^ (2 * k)]
-        send[k] = grams[lax.axis_index("pix") ^ (2 * k + 1)]
-    near = pl.multiple_of((lax.axis_index("spec") & 1) * half, LANES)
-    far = pl.multiple_of(half - near, LANES)
-    own[0] = weights[:, pl.ds(near, half)]
-    own[1] = flux[:, pl.ds(near, half)]
-    other[0] = weights[:, pl.ds(far, half)]
-    other[1] = flux[:, pl.ds(far, half)]
-
-
-def fold_kernel(keep, arrived, *outs):
-    for k, out in enumerate(outs):
-        out[...] = keep[k] + arrived[k]
-
-
-def coeff_kernel(*refs, rank, chunk):
-    parts, (out, packed, full, scaled) = refs[:-4], refs[-4:]
-    total = parts[0][...]
-    for part in parts[1:]:
-        total = total + part[...]
+    for k in range(grams.shape[0] // span):
+        for m, send in enumerate(sends):
+            send[k] = grams[pixel_place() ^ (span * k + m)]
+    for copy in copies[3:]:
+        copy.wait()
+
+
+def add_kernel(*refs, flip):
+    for h in range(refs[0].shape[0]):
+        total = refs[0][h]
+        for term in refs[1:-1]:
+            total = total + term[h ^ flip]
+        refs[-1][h] = total
+
+
+def coeff_kernel(sums, arrived, out, packed, full, scaled, *, rank, chunk):
+    chunks = sums.shape[0]
+    total = [sums[h] + arrived[h ^ (chunks // 2)] for h in range(chunks)]
     rows, whole, rest, beside, _ = layout(rank, chunk)
-    filler = jnp.ones((LANES - rows, LANES), jnp.float32)
-    blocks = [total[k * rows : (k + 1) * rows] for k in range(whole)]
+    filler = jnp.ones((LANES - chunks * rows, LANES), jnp.float32)
+    for t in range(whole):
+        block = [total[h][t * rows : (t + 1) * rows] for h in range(chunks)]
+        packed[t * LANES : (t + 1) * LANES, :] = jnp.concatenate(block + [filler], axis=0).T
     groups = []
-    for g in range(rows // ROWS):
-        base = rows * whole + g // beside * ROWS
-        group = total[base : base + ROWS]
-        groups.append(pltpu.roll(group, LANES - g % beside * rest, 1) if g % beside else group)
-    blocks.append(jnp.concatenate(groups, axis=0))
-    for k, block in enumerate(blocks):
-        packed[k * LANES : (k + 1) * LANES, :] = jnp.concatenate([block, filler], axis=0).T
+    for h in range(chunks):
+        for g in range(rows // ROWS):
+            base = rows * whole + g // beside * ROWS
+            group = total[h][base : base + ROWS]
+            groups.append(pltpu.roll(group, LANES - g % beside * rest, 1) if g % beside else group)
+    packed[whole * LANES :, :] = jnp.concatenate(groups + [filler], axis=0).T
     lead = pair_rows(rank)
     unpack(packed, full, rank)
     (solved,) = solve([full], [packed[lead : lead + rank, :]], [scaled], rank)
     lane = lax.broadcasted_iota(jnp.int32, (ROWS, LANES), 1)
-    tile = jnp.zeros((ROWS, LANES), jnp.float32)
-    for a in range(rank // ROWS):
-        part = solved[a * ROWS : (a + 1) * ROWS, :]
-        if a:
-            part = pltpu.roll(part, a * chunk, 1)
-        tile = jnp.where((lane >= a * chunk) & (lane < (a + 1) * chunk), part, tile)
-    for k in range(out.shape[0]):
-        out[k] = tile
-
-
-def pixel_kernel(tiles, *rest, peers, rank, chunk):
-    picks, (out, twice, pairs, high, low, full, scaled) = rest[:peers], rest[peers:]
+    for h in range(chunks):
+        tile = jnp.zeros((ROWS, LANES), jnp.float32)
+        for a in range(rank // ROWS):
+            part = solved[a * ROWS : (a + 1) * ROWS, :]
+            shift = (a * chunk - h * rows) % LANES
+            if shift:
+                part = pltpu.roll(part, shift, 1)
+            tile = jnp.where((lane >= a * chunk) & (lane < (a + 1) * chunk), part, tile)
+        for k in range(out.shape[0]):
+            out[k, h] = tile
+
+
+def terms_kernel(*refs, peers):
+    picks, (high, low) = refs[:peers], refs[peers:]
     spectra = picks[0].shape[1]
-    half = picks[0].shape[2]
+    for q, pick in enumerate(picks):
+        rows = pl.ds(pl.multiple_of((lax.axis_index("spec") ^ q) * spectra, 16), spectra)
+        high[0, rows, :], low[0, rows, :] = halves(pick[0])
+        high[1, rows, :], low[1, rows, :] = halves(pick[0] * pick[1])
+
+
+def pixel_kernel(tiles, high, low, out, twice, pairs, full, scaled, *, peers, rank, chunk):
+    spectra = high.shape[1] // peers
+    half = high.shape[2]
     group = spectra // chunk
     lane = lax.broadcasted_iota(jnp.int32, (ROWS, LANES), 1)
     width = twice.shape[1]
-    for q in range(peers):
-        rows = slice(q * spectra, (q + 1) * spectra)
-        for k in range(2):
-            high[k, rows, :], low[k, rows, :] = halves(picks[q][k])
     for a in range(rank // ROWS):
         columns = [jnp.zeros((ROWS, LANES), jnp.float32) for _ in range(width // LANES)]
         for q in range(peers):
             for k in range(group):
-                part = tiles[(lax.axis_index("spec") ^ q) * group + k]
+                near = pixel_place() ^ k
+                part = tiles[q * SPAN + k % SPAN, near // SPAN]
                 start = q * spectra + k * chunk
                 shift = (start - a * chunk) % LANES
                 if shift:
@@ -250,11 +263,12 @@
     inputs = [pltpu.with_memory_space_constraint(a, pltpu.HBM) for a in (spectra_flux, pixel_weights, old_basis)]
 
     def swap(value, axis, mask):
-        return lax.ppermute(value, axis, [(s, s ^ mask) for s in range(peers if axis == "spec" else groups)])
-
-    keep, send, own, other = call(
-        functools.partial(spec_kernel, chunk=chunk),
-        [shape(groups // 2, rows, LANES)] * 2 + [shape(2, spectra, half)] * 2,
+        axis, size = ("spec", peers) if axis == "spec" else (("high", "low"), groups)
+        return lax.ppermute(value, axis, [(s, s ^ mask) for s in range(size)])
+
+    own, other, *sends = call(
+        functools.partial(spec_kernel, chunk=chunk, span=SPAN),
+        [shape(2, spectra, half)] * 2 + [shape(groups // SPAN, rows, LANES)] * SPAN,
         [
             (spectra, pixels),
             (spectra, pixels),
@@ -266,41 +280,50 @@
             (half_type, 2 * rank, pixels),
             (spectra, LANES),
             (groups, rows, LANES),
-            pltpu.SemaphoreType.DMA((3,)),
+            pltpu.SemaphoreType.DMA((7,)),
         ],
         *inputs,
         space=pl.ANY,
     )
-    arrived = swap(send, "pix", 1)
+    arrived = [swap(sends[m], "pix", m) for m in range(SPAN - 1, 0, -1)]
     picks = [own] + [swap(other if q & 1 else own, "spec", q) for q in range(1, peers)]
-    sums = call(fold_kernel, [shape(rows, LANES)] * (groups // 2), [], keep, arrived)
-    parts = [sums[0]] + [swap(sums[k], "pix", 2 * k) for k in range(1, groups // 2)]
+    kept = shape(*sends[0].shape)
+    sums = call(functools.partial(add_kernel, flip=0), kept, [], sends[0], *arrived)
+    reach = SPAN
+    while 2 * reach < groups:
+        sums = call(functools.partial(add_kernel, flip=reach // SPAN), kept, [], sums, swap(sums, "pix", reach))
+        reach *= 2
     tiles = call(
         functools.partial(coeff_kernel, rank=rank, chunk=chunk),
-        shape(peers * groups, ROWS, LANES),
+        shape(peers * SPAN, groups // SPAN, ROWS, LANES),
         [(wide, LANES), (rank * rank, LANES), (rank * rank, LANES)],
-        *parts,
-    )
-    tiles = lax.all_to_all(tiles, ("spec", "pix"), 0, 0)
+        sums,
+        swap(sums, "pix", reach),
+    )
+    tiles = lax.all_to_all(tiles, ("spec", "low"), 0, 0)
     depth = peers * spectra
+    terms = [jax.ShapeDtypeStruct((2, depth, half), jnp.bfloat16)] * 2
+    high, low = call(functools.partial(terms_kernel, peers=peers), terms, [], *picks)
     mine = call(
         functools.partial(pixel_kernel, peers=peers, rank=rank, chunk=chunk),
         shape(rank, half),
         [
             (2 * rank, up(depth, LANES)),
             (half_type, 2 * lead, up(depth, LANES)),
-            (half_type, 2, depth, half),
-            (half_type, 2, depth, half),
             (half // LANES, rank * rank, LANES),
             (half // LANES, rank * rank, LANES),
         ],
         tiles,
-        *picks,
+        high,
+        low,
     )
     return call(place_kernel, shape(rank, pixels), [], mine, swap(mine, "spec", 1))
 
 
 def solution(mesh):
-    placed = (P("spec", "pix"), P("spec", "pix"), P(None, "pix"))
-    body = functools.partial(local, mesh.shape["spec"], mesh.shape["pix"])
-    return jax.shard_map(body, mesh=mesh, in_specs=placed, out_specs=P(None, "pix"), check_vma=False)
+    peers, groups = mesh.shape["spec"], mesh.shape["pix"]
+    split = jax.sharding.Mesh(mesh.devices.reshape(peers, groups // SPAN, SPAN), ("spec", "high", "low"))
+    pix = ("high", "low")
+    body = functools.partial(local, peers, groups)
+    placed = (P("spec", pix), P("spec", pix), P(None, pix))
+    return jax.shard_map(body, mesh=split, in_specs=placed, out_specs=P(None, pix), check_vma=False)

time: 41.1 us -> 36.3 us (0.88)
  starting transfers between devices: 18.7 us -> 13.7 us
    ppermute x8, starting transfers between devices: 13.1 us -> 9.42 us  [swap(): return lax.ppermute(value, axis, [(s, s ^ mask) for s in range(size)])]
    all_to_all x1, waiting for transfers between devices: 7.71 us -> 5.8 us  [local(): tiles = lax.all_to_all(tiles, ('spec', 'low'), 0, 0)]
    ppermute x8, waiting for transfers between devices: 7.49 us -> 9.32 us  [swap(): return lax.ppermute(value, axis, [(s, s ^ mask) for s in range(size)])]
    all_to_all x1, starting transfers between devices: 5.56 us -> 4.28 us  [local(): tiles = lax.all_to_all(tiles, ('spec', 'low'), 0, 0)]
    pallas_call x5 -> x6, Pallas kernels: 6.93 us -> 7.19 us  [call(): pl.pallas_call(kernel, out_shape=outs, in_specs=[pl.BlockSpec(memory_spac...]
  transfers between devices with their start and end apart: 9 -> 9, of which waited for: 6 -> 5; matrix products, arithmetic and copies ran while one was open for 0% -> 0% of each run, Pallas kernels for 4% -> 5%
where the time goes in v3:
time: 36.3 us; the launch traced here: 36.1 us
  waiting for transfers between devices  15.1 us (42%)
  starting transfers between devices  13.7 us (38%)
  Pallas kernels  7.19 us (20%)
    ppermute x8, starting transfers between devices, swap(): return lax.ppermute(value, axis, [(s, s ^ mask) for s in range(size)])  9.42 us
    ppermute x8, waiting for transfers between devices, swap(): return lax.ppermute(value, axis, [(s, s ^ mask) for s in range(size)])  9.32 us
    pallas_call x6, Pallas kernels, call(): pl.pallas_call(kernel, out_shape=outs, in_specs=[pl.BlockSpec(memory_spac...  7.19 us
    all_to_all x1, waiting for transfers between devices, local(): tiles = lax.all_to_all(tiles, ('spec', 'low'), 0, 0)  5.8 us
    all_to_all x1, starting transfers between devices, local(): tiles = lax.all_to_all(tiles, ('spec', 'low'), 0, 0)  4.28 us
  transfers between devices with their start and end apart: 9, of which 5 were waited for; matrix products, arithmetic and copies ran while one was open for 0% of the time, Pallas kernels for 5%

profile of v3, /device:TPU:0, one launch (start us, length us, event | category | flops | bytes accessed | tf_op | source)
XLA Modules:
  0.0 36.1 jit_solution(13247764654957006057)
XLA Ops:
  0.0 2.5 %shard_map.37 = (f32[2,192,256]{2,1,0:T(8,128)S(1)}, f32[2,192,256]{2,1,0:T(8,128)S(1)}, f32[2,112,128]{2,1,0:T(8,128)S(1)}, f32[2,112,128]{2,1,0:T(8,128)S(1)},...) custom-call(f32[192,512]{1,0:T(8,128)} %flux_hbm.1, f32[192,512]{1,0:T(8,128)} %weights_hbm.1, f32[32,512]{1,0:T(8,128)} %basis_hbm.1), custom_call_target="tpu_custom_call" | custom-call | tf_op jit(solution)/shard_map/pallas_call | solution.py:241
  2.5 4.0 %collective-permute-start = (f32[2,112,128]{2,1,0:T(8,128)S(1)}, f32[2,112,128]{2,1,0:T(8,128)S(1)}, u32[]{:S(2)}, u32[]{:S(2)}) collective-permute-start(f32[2,112,128]{2,1,0:T(8,128)S(1)} %get-tuple-element.14), channel_id=1, source_target_pairs={{0,3},{1,2},{2,1},{3,0},{4,7},{5,6},{6,5},{7,4},{8,11},{9,10},{10,... | collective-permute-start | bytes 344072 | tf_op jit(solution)/shard_map/ppermute | solution.py:267
  6.5 0.5 %collective-permute-start.1 = (f32[2,112,128]{2,1,0:T(8,128)S(1)}, f32[2,112,128]{2,1,0:T(8,128)S(1)}, u32[]{:S(2)}, u32[]{:S(2)}) collective-permute-start(f32[2,112,128]{2,1,0:T(8,128)S(1)} %get-tuple-element.15), channel_id=1, source_target_pairs={{0,2},{1,3},{2,0},{3,1},{4,6},{5,7},{6,4},{7,5},{8,10},{9,11},{10,... | collective-permute-start | bytes 344072 | tf_op jit(solution)/shard_map/ppermute | solution.py:267
  6.9 0.2 collective-permute-start.2
  7.1 1.9 %collective-permute-start.5 = (f32[2,192,256]{2,1,0:T(8,128)S(1)}, f32[2,192,256]{2,1,0:T(8,128)S(1)}, u32[]{:S(2)}, u32[]{:S(2)}) collective-permute-start(f32[2,192,256]{2,1,0:T(8,128)S(1)} %get-tuple-element.17.refs_0_), channel_id=1, source_target_pairs={{0,16},{8,24},{16,0},{24,8},{1,17},{9,25},{17,1},{25,9},{2,18},{10... | collective-permute-start | bytes 1179656 | tf_op jit(solution)/shard_map/ppermute | solution.py:267
  9.0 0.0 collective-permute-start.6
  9.0 1.5 %collective-permute-done.refs_1_ = f32[2,112,128]{2,1,0:T(8,128)S(1)} collective-permute-done((f32[2,112,128]{2,1,0:T(8,128)S(1)}, f32[2,112,128]{2,1,0:T(8,128)S(1)}, u32[]{:S(2)}, u32[]{:S(2)}) %collective-permute-start) | collective-permute-done | bytes 114720 | tf_op jit(solution)/shard_map/ppermute | solution.py:267
  10.5 0.0 collective-permute-start.4
  10.5 1.8 %collective-permute-done.1.refs_2_ = f32[2,112,128]{2,1,0:T(8,128)S(1)} collective-permute-done((f32[2,112,128]{2,1,0:T(8,128)S(1)}, f32[2,112,128]{2,1,0:T(8,128)S(1)}, u32[]{:S(2)}, u32[]{:S(2)}) %collective-permute-start.1) | collective-permute-done | bytes 114720 | tf_op jit(solution)/shard_map/ppermute | solution.py:267
  12.3 0.0 collective-permute-done.2.refs_3_
  12.3 2.7 %collective-permute-start.3 = (f32[2,112,128]{2,1,0:T(8,128)S(1)}, f32[2,112,128]{2,1,0:T(8,128)S(1)}, u32[]{:S(2)}, u32[]{:S(2)}) collective-permute-start(f32[2,112,128]{2,1,0:T(8,128)S(1)} %shard_map.38.sums), channel_id=1, source_target_pairs={{0,4},{1,5},{2,6},{3,7},{4,0},{5,1},{6,2},{7,3},{8,12},{9,13},{10,... | collective-permute-start | bytes 344072 | tf_op jit(solution)/shard_map/ppermute | solution.py:267
  15.0 5.0 %collective-permute-done.3.arrived = f32[2,112,128]{2,1,0:T(8,128)S(1)} collective-permute-done((f32[2,112,128]{2,1,0:T(8,128)S(1)}, f32[2,112,128]{2,1,0:T(8,128)S(1)}, u32[]{:S(2)}, u32[]{:S(2)}) %collective-permute-start.3) | collective-permute-done | bytes 114720 | tf_op jit(solution)/shard_map/ppermute | solution.py:267
  20.0 1.5 %shard_map.39 = f32[16,2,8,128]{3,2,1,0:T(8,128)} custom-call(f32[2,112,128]{2,1,0:T(8,128)S(1)} %shard_map.38.sums, f32[2,112,128]{2,1,0:T(8,128)S(1)} %collective-permute-done.3.arrived), custom_call_target="tpu_custom_call" | custom-call | tf_op jit(solution)/shard_map/pallas_call | solution.py:241
  21.5 4.3 %all-to-all-start = ((f32[16,2,8,128]{3,2,1,0:T(8,128)}), f32[16,2,8,128]{3,2,1,0:T(8,128)S(1)}, u32[]{:S(2)}, u32[]{:S(2)}) async-start(f32[16,2,8,128]{3,2,1,0:T(8,128)} %shard_map.39), calls=%async_computation | async-start | bytes 262144 | tf_op jit(solution)/shard_map/all_to_all | solution.py:303
  25.8 0.0 collective-permute-done.5.refs_2_
  25.8 0.0 collective-permute-done.6.refs_3_
  25.8 0.0 collective-permute-done.4.refs_1_
  25.8 0.2 shard_map.40
  26.0 5.8 %all-to-all-done.tiles = f32[16,2,8,128]{3,2,1,0:T(8,128)S(1)} async-done(((f32[16,2,8,128]{3,2,1,0:T(8,128)}), f32[16,2,8,128]{3,2,1,0:T(8,128)S(1)}, u32[]{:S(2)}, u32[]{:S(2)}) %all-to-all-start) | async-done | bytes 131104 | tf_op jit(solution)/shard_map/all_to_all | solution.py:303
  31.8 2.3 %shard_map.41.own = f32[32,256]{1,0:T(8,128)S(1)} custom-call(f32[16,2,8,128]{3,2,1,0:T(8,128)S(1)} %all-to-all-done.tiles, bf16[2,768,256]{2,1,0:T(8,128)(2,1)S(1)} %get-tuple-element.19.high, bf16[2,768,256]{2,1,0:T(8,128)(2,1)S(1)} %get-tuple-element.20.low), custom_call_target="tpu_custom_call" | custom-call | tf_op jit(solution)/shard_map/pallas_call | solution.py:241
  34.2 0.2 collective-permute-start.7
  34.3 1.1 %collective-permute-done.7.other = f32[32,256]{1,0:T(8,128)S(1)} collective-permute-done((f32[32,256]{1,0:T(8,128)S(1)}, f32[32,256]{1,0:T(8,128)S(1)}, u32[]{:S(2)}, u32[]{:S(2)}) %collective-permute-start.7) | collective-permute-done | bytes 32800 | tf_op jit(solution)/shard_map/ppermute | solution.py:267
  35.4 0.6 %shard_map.42 = f32[32,512]{1,0:T(8,128)} custom-call(f32[32,256]{1,0:T(8,128)S(1)} %shard_map.41.own, f32[32,256]{1,0:T(8,128)S(1)} %collective-permute-done.7.other), custom_call_target="tpu_custom_call" | custom-call | tf_op jit(solution)/shard_map/pallas_call | solution.py:241
  (1 shorter events, 0.0 us)
Async XLA Ops:
  2.5 8.0 %collective-permute-start = (f32[2,112,128]{2,1,0:T(8,128)S(1)}, f32[2,112,128]{2,1,0:T(8,128)S(1)}, u32[]{:S(2)}, u32[]{:S(2)}) collective-permute-start(f32[2,112,128]{2,1,0:T(8,128)S(1)} %get-tuple-element.14), channel_id=1, source_target_pairs={{0,3},{1,2},{2,1},{3,0},{4,7},{5,6},{6,5},{7,4},{8,11},{9,10},{10,... | collective-permute-start | bytes 344072 | tf_op jit(solution)/shard_map/ppermute | solution.py:267
  6.5 5.8 %collective-permute-start.1 = (f32[2,112,128]{2,1,0:T(8,128)S(1)}, f32[2,112,128]{2,1,0:T(8,128)S(1)}, u32[]{:S(2)}, u32[]{:S(2)}) collective-permute-start(f32[2,112,128]{2,1,0:T(8,128)S(1)} %get-tuple-element.15), channel_id=1, source_target_pairs={{0,2},{1,3},{2,0},{3,1},{4,6},{5,7},{6,4},{7,5},{8,10},{9,11},{10,... | collective-permute-start | bytes 344072 | tf_op jit(solution)/shard_map/ppermute | solution.py:267
  6.9 5.3 %collective-permute-start.2 = (f32[2,112,128]{2,1,0:T(8,128)S(1)}, f32[2,112,128]{2,1,0:T(8,128)S(1)}, u32[]{:S(2)}, u32[]{:S(2)}) collective-permute-start(f32[2,112,128]{2,1,0:T(8,128)S(1)} %get-tuple-element.16), channel_id=1, source_target_pairs={{0,1},{1,0},{2,3},{3,2},{4,5},{5,4},{6,7},{7,6},{8,9},{9,8},{10,11... | collective-permute-start | bytes 344072 | tf_op jit(solution)/shard_map/ppermute | solution.py:267
  7.1 18.6 %collective-permute-start.5 = (f32[2,192,256]{2,1,0:T(8,128)S(1)}, f32[2,192,256]{2,1,0:T(8,128)S(1)}, u32[]{:S(2)}, u32[]{:S(2)}) collective-permute-start(f32[2,192,256]{2,1,0:T(8,128)S(1)} %get-tuple-element.17.refs_0_), channel_id=1, source_target_pairs={{0,16},{8,24},{16,0},{24,8},{1,17},{9,25},{17,1},{25,9},{2,18},{10... | collective-permute-start | bytes 1179656 | tf_op jit(solution)/shard_map/ppermute | solution.py:267
  9.0 16.8 %collective-permute-start.6 = (f32[2,192,256]{2,1,0:T(8,128)S(1)}, f32[2,192,256]{2,1,0:T(8,128)S(1)}, u32[]{:S(2)}, u32[]{:S(2)}) collective-permute-start(f32[2,192,256]{2,1,0:T(8,128)S(1)} %get-tuple-element.18), channel_id=1, source_target_pairs={{0,24},{8,16},{16,8},{24,0},{1,25},{9,17},{17,9},{25,1},{2,26},{10... | collective-permute-start | bytes 1179656 | tf_op jit(solution)/shard_map/ppermute | solution.py:267
  10.5 15.3 %collective-permute-start.4 = (f32[2,192,256]{2,1,0:T(8,128)S(1)}, f32[2,192,256]{2,1,0:T(8,128)S(1)}, u32[]{:S(2)}, u32[]{:S(2)}) collective-permute-start(f32[2,192,256]{2,1,0:T(8,128)S(1)} %get-tuple-element.18), channel_id=1, source_target_pairs={{0,8},{8,0},{16,24},{24,16},{1,9},{9,1},{17,25},{25,17},{2,10},{10... | collective-permute-start | bytes 1179656 | tf_op jit(solution)/shard_map/ppermute | solution.py:267
  12.3 7.7 %collective-permute-start.3 = (f32[2,112,128]{2,1,0:T(8,128)S(1)}, f32[2,112,128]{2,1,0:T(8,128)S(1)}, u32[]{:S(2)}, u32[]{:S(2)}) collective-permute-start(f32[2,112,128]{2,1,0:T(8,128)S(1)} %shard_map.38.sums), channel_id=1, source_target_pairs={{0,4},{1,5},{2,6},{3,7},{4,0},{5,1},{6,2},{7,3},{8,12},{9,13},{10,... | collective-permute-start | bytes 344072 | tf_op jit(solution)/shard_map/ppermute | solution.py:267
  21.5 10.4 %all-to-all-start = ((f32[16,2,8,128]{3,2,1,0:T(8,128)}), f32[16,2,8,128]{3,2,1,0:T(8,128)S(1)}, u32[]{:S(2)}, u32[]{:S(2)}) async-start(f32[16,2,8,128]{3,2,1,0:T(8,128)} %shard_map.39), calls=%async_computation | async-start | bytes 262144 | tf_op jit(solution)/shard_map/all_to_all | solution.py:303
  34.2 1.3 %collective-permute-start.7 = (f32[32,256]{1,0:T(8,128)S(1)}, f32[32,256]{1,0:T(8,128)S(1)}, u32[]{:S(2)}, u32[]{:S(2)}) collective-permute-start(f32[32,256]{1,0:T(8,128)S(1)} %shard_map.41.own), channel_id=1, source_target_pairs={{0,8},{8,0},{16,24},{24,16},{1,9},{9,1},{17,25},{25,17},{2,10},{10... | collective-permute-start | bytes 98312 | tf_op jit(solution)/shard_map/ppermute | solution.py:267

commit v4 on v3

--- a/solution.py
+++ b/solution.py
@@ -55,20 +55,47 @@
 
 
 def solve(fulls, targets, scaleds, rank):
-    row = lax.broadcasted_iota(jnp.int32, targets[0].shape, 0)
-    targets, pivots = list(targets), [jnp.zeros_like(target) for target in targets]
+    row = lax.broadcasted_iota(jnp.int32, (ROWS, LANES), 0)
+    blocks = rank // ROWS
+    targets = [[target[b * ROWS : (b + 1) * ROWS, :] for b in range(blocks)] for target in targets]
+    pivots = [[jnp.zeros((ROWS, LANES), jnp.float32) for _ in range(blocks)] for _ in targets]
+    tiles = range(len(targets))
+
+    def part(k, b):
+        return slice(k * rank + b * ROWS, k * rank + (b + 1) * ROWS)
+
+    def reduced(t, k, b, stop):
+        value = fulls[t][part(k, b), :]
+        for j in range(stop):
+            value = value - scaleds[t][part(j, b), :] * fulls[t][j * rank + k : j * rank + k + 1, :]
+        return value
+
     for k in range(rank):
-        here = row == k
-        for t, (full, scaled) in enumerate(zip(fulls, scaleds)):
-            column = full[k * rank : (k + 1) * rank, :]
-            for j in range(k):
-                column = column - scaled[j * rank : (j + 1) * rank, :] * full[j * rank + k : j * rank + k + 1, :]
-            full[k * rank : (k + 1) * rank, :] = column
-            factor = jnp.where(here, 0.0, column * (1.0 / column[k : k + 1, :]))
-            scaled[k * rank : (k + 1) * rank, :] = factor
-            pivots[t] = jnp.where(here, column, pivots[t])
-            targets[t] = targets[t] - factor * targets[t][k : k + 1, :]
-    return [target / pivot for target, pivot in zip(targets, pivots)]
+        first, place = k // ROWS, k % ROWS
+        here = row == place
+        for t in tiles:
+            column = [reduced(t, k, b, k) for b in range(first, blocks)]
+            inverse = 1.0 / column[0][place : place + 1, :]
+            pivots[t][first] = jnp.where(here, column[0], pivots[t][first])
+            known = targets[t][first][place : place + 1, :]
+            for b in range(first, blocks):
+                fulls[t][part(k, b), :] = column[b - first]
+                factor = column[b - first] * inverse
+                if b == first:
+                    factor = jnp.where(here, 0.0, factor)
+                scaleds[t][part(k, b), :] = factor
+                targets[t][b] = targets[t][b] - factor * known
+        if place == ROWS - 1:
+            for t in tiles:
+                for later in range(k + 1, rank):
+                    fulls[t][part(later, first), :] = reduced(t, later, first, k + 1)
+    for b in reversed(range(blocks)):
+        for t in tiles:
+            for k in reversed(range((b + 1) * ROWS, rank)):
+                known = targets[t][k // ROWS][k % ROWS : k % ROWS + 1, :]
+                targets[t][b] = targets[t][b] - fulls[t][part(k, b), :] * known
+            targets[t][b] = targets[t][b] / pivots[t][b]
+    return [jnp.concatenate(target, axis=0) for target in targets]
 
 
 def dot(left, right, right_axis):

time: 36.3 us -> 36.1 us (level)
  no operation moved by 1% of the time
where the time goes in v4:
time: 36.1 us; the launch traced here: 35.8 us
  waiting for transfers between devices  15.1 us (42%)
  starting transfers between devices  13.7 us (38%)
  Pallas kernels  6.95 us (19%)
    ppermute x8, starting transfers between devices, swap(): return lax.ppermute(value, axis, [(s, s ^ mask) for s in range(size)])  9.43 us
    ppermute x8, waiting for transfers between devices, swap(): return lax.ppermute(value, axis, [(s, s ^ mask) for s in range(size)])  9.31 us
    pallas_call x6, Pallas kernels, call(): pl.pallas_call(kernel, out_shape=outs, in_specs=[pl.BlockSpec(memory_spac...  6.95 us
    all_to_all x1, waiting for transfers between devices, local(): tiles = lax.all_to_all(tiles, ('spec', 'low'), 0, 0)  5.8 us
    all_to_all x1, starting transfers between devices, local(): tiles = lax.all_to_all(tiles, ('spec', 'low'), 0, 0)  4.28 us
  transfers between devices with their start and end apart: 9, of which 5 were waited for; matrix products, arithmetic and copies ran while one was open for 0% of the time, Pallas kernels for 5%

profile of v4, /device:TPU:0, one launch (start us, length us, event | category | flops | bytes accessed | tf_op | source)
XLA Modules:
  0.0 35.8 jit_solution(13722287119383727643)
XLA Ops:
  0.0 2.5 %shard_map.37 = (f32[2,192,256]{2,1,0:T(8,128)S(1)}, f32[2,192,256]{2,1,0:T(8,128)S(1)}, f32[2,112,128]{2,1,0:T(8,128)S(1)}, f32[2,112,128]{2,1,0:T(8,128)S(1)},...) custom-call(f32[192,512]{1,0:T(8,128)} %flux_hbm.1, f32[192,512]{1,0:T(8,128)} %weights_hbm.1, f32[32,512]{1,0:T(8,128)} %basis_hbm.1), custom_call_target="tpu_custom_call" | custom-call | tf_op jit(solution)/shard_map/pallas_call | solution.py:268
  2.5 4.0 %collective-permute-start = (f32[2,112,128]{2,1,0:T(8,128)S(1)}, f32[2,112,128]{2,1,0:T(8,128)S(1)}, u32[]{:S(2)}, u32[]{:S(2)}) collective-permute-start(f32[2,112,128]{2,1,0:T(8,128)S(1)} %get-tuple-element.14), channel_id=1, source_target_pairs={{0,3},{1,2},{2,1},{3,0},{4,7},{5,6},{6,5},{7,4},{8,11},{9,10},{10,... | collective-permute-start | bytes 344072 | tf_op jit(solution)/shard_map/ppermute | solution.py:294
  6.5 0.5 %collective-permute-start.1 = (f32[2,112,128]{2,1,0:T(8,128)S(1)}, f32[2,112,128]{2,1,0:T(8,128)S(1)}, u32[]{:S(2)}, u32[]{:S(2)}) collective-permute-start(f32[2,112,128]{2,1,0:T(8,128)S(1)} %get-tuple-element.15), channel_id=1, source_target_pairs={{0,2},{1,3},{2,0},{3,1},{4,6},{5,7},{6,4},{7,5},{8,10},{9,11},{10,... | collective-permute-start | bytes 344072 | tf_op jit(solution)/shard_map/ppermute | solution.py:294
  6.9 0.2 collective-permute-start.2
  7.1 1.9 %collective-permute-start.5 = (f32[2,192,256]{2,1,0:T(8,128)S(1)}, f32[2,192,256]{2,1,0:T(8,128)S(1)}, u32[]{:S(2)}, u32[]{:S(2)}) collective-permute-start(f32[2,192,256]{2,1,0:T(8,128)S(1)} %get-tuple-element.17.refs_0_), channel_id=1, source_target_pairs={{0,16},{8,24},{16,0},{24,8},{1,17},{9,25},{17,1},{25,9},{2,18},{10... | collective-permute-start | bytes 1179656 | tf_op jit(solution)/shard_map/ppermute | solution.py:294
  9.0 0.0 collective-permute-start.6
  9.0 1.5 %collective-permute-done.refs_1_ = f32[2,112,128]{2,1,0:T(8,128)S(1)} collective-permute-done((f32[2,112,128]{2,1,0:T(8,128)S(1)}, f32[2,112,128]{2,1,0:T(8,128)S(1)}, u32[]{:S(2)}, u32[]{:S(2)}) %collective-permute-start) | collective-permute-done | bytes 114720 | tf_op jit(solution)/shard_map/ppermute | solution.py:294
  10.5 0.0 collective-permute-start.4
  10.5 1.8 %collective-permute-done.1.refs_2_ = f32[2,112,128]{2,1,0:T(8,128)S(1)} collective-permute-done((f32[2,112,128]{2,1,0:T(8,128)S(1)}, f32[2,112,128]{2,1,0:T(8,128)S(1)}, u32[]{:S(2)}, u32[]{:S(2)}) %collective-permute-start.1) | collective-permute-done | bytes 114720 | tf_op jit(solution)/shard_map/ppermute | solution.py:294
  12.3 0.0 collective-permute-done.2.refs_3_
  12.3 2.7 %collective-permute-start.3 = (f32[2,112,128]{2,1,0:T(8,128)S(1)}, f32[2,112,128]{2,1,0:T(8,128)S(1)}, u32[]{:S(2)}, u32[]{:S(2)}) collective-permute-start(f32[2,112,128]{2,1,0:T(8,128)S(1)} %shard_map.38.sums), channel_id=1, source_target_pairs={{0,4},{1,5},{2,6},{3,7},{4,0},{5,1},{6,2},{7,3},{8,12},{9,13},{10,... | collective-permute-start | bytes 344072 | tf_op jit(solution)/shard_map/ppermute | solution.py:294
  15.0 5.0 %collective-permute-done.3.arrived = f32[2,112,128]{2,1,0:T(8,128)S(1)} collective-permute-done((f32[2,112,128]{2,1,0:T(8,128)S(1)}, f32[2,112,128]{2,1,0:T(8,128)S(1)}, u32[]{:S(2)}, u32[]{:S(2)}) %collective-permute-start.3) | collective-permute-done | bytes 114720 | tf_op jit(solution)/shard_map/ppermute | solution.py:294
  20.0 1.4 %shard_map.39 = f32[16,2,8,128]{3,2,1,0:T(8,128)} custom-call(f32[2,112,128]{2,1,0:T(8,128)S(1)} %shard_map.38.sums, f32[2,112,128]{2,1,0:T(8,128)S(1)} %collective-permute-done.3.arrived), custom_call_target="tpu_custom_call" | custom-call | tf_op jit(solution)/shard_map/pallas_call | solution.py:268
  21.4 4.3 %all-to-all-start = ((f32[16,2,8,128]{3,2,1,0:T(8,128)}), f32[16,2,8,128]{3,2,1,0:T(8,128)S(1)}, u32[]{:S(2)}, u32[]{:S(2)}) async-start(f32[16,2,8,128]{3,2,1,0:T(8,128)} %shard_map.39), calls=%async_computation | async-start | bytes 262144 | tf_op jit(solution)/shard_map/all_to_all | solution.py:330
  25.7 0.0 collective-permute-done.5.refs_2_
  25.7 0.0 collective-permute-done.6.refs_3_
  25.7 0.0 collective-permute-done.4.refs_1_
  25.7 0.2 shard_map.40
  26.0 5.8 %all-to-all-done.tiles = f32[16,2,8,128]{3,2,1,0:T(8,128)S(1)} async-done(((f32[16,2,8,128]{3,2,1,0:T(8,128)}), f32[16,2,8,128]{3,2,1,0:T(8,128)S(1)}, u32[]{:S(2)}, u32[]{:S(2)}) %all-to-all-start) | async-done | bytes 131104 | tf_op jit(solution)/shard_map/all_to_all | solution.py:330
  31.8 2.2 %shard_map.41.own = f32[32,256]{1,0:T(8,128)S(1)} custom-call(f32[16,2,8,128]{3,2,1,0:T(8,128)S(1)} %all-to-all-done.tiles, bf16[2,768,256]{2,1,0:T(8,128)(2,1)S(1)} %get-tuple-element.19.high, bf16[2,768,256]{2,1,0:T(8,128)(2,1)S(1)} %get-tuple-element.20.low), custom_call_target="tpu_custom_call" | custom-call | tf_op jit(solution)/shard_map/pallas_call | solution.py:268
  33.9 0.2 collective-permute-start.7
  34.1 1.1 %collective-permute-done.7.other = f32[32,256]{1,0:T(8,128)S(1)} collective-permute-done((f32[32,256]{1,0:T(8,128)S(1)}, f32[32,256]{1,0:T(8,128)S(1)}, u32[]{:S(2)}, u32[]{:S(2)}) %collective-permute-start.7) | collective-permute-done | bytes 32800 | tf_op jit(solution)/shard_map/ppermute | solution.py:294
  35.2 0.6 %shard_map.42 = f32[32,512]{1,0:T(8,128)} custom-call(f32[32,256]{1,0:T(8,128)S(1)} %shard_map.41.own, f32[32,256]{1,0:T(8,128)S(1)} %collective-permute-done.7.other), custom_call_target="tpu_custom_call" | custom-call | tf_op jit(solution)/shard_map/pallas_call | solution.py:268
  (1 shorter events, 0.0 us)
Async XLA Ops:
  2.5 8.0 %collective-permute-start = (f32[2,112,128]{2,1,0:T(8,128)S(1)}, f32[2,112,128]{2,1,0:T(8,128)S(1)}, u32[]{:S(2)}, u32[]{:S(2)}) collective-permute-start(f32[2,112,128]{2,1,0:T(8,128)S(1)} %get-tuple-element.14), channel_id=1, source_target_pairs={{0,3},{1,2},{2,1},{3,0},{4,7},{5,6},{6,5},{7,4},{8,11},{9,10},{10,... | collective-permute-start | bytes 344072 | tf_op jit(solution)/shard_map/ppermute | solution.py:294
  6.5 5.8 %collective-permute-start.1 = (f32[2,112,128]{2,1,0:T(8,128)S(1)}, f32[2,112,128]{2,1,0:T(8,128)S(1)}, u32[]{:S(2)}, u32[]{:S(2)}) collective-permute-start(f32[2,112,128]{2,1,0:T(8,128)S(1)} %get-tuple-element.15), channel_id=1, source_target_pairs={{0,2},{1,3},{2,0},{3,1},{4,6},{5,7},{6,4},{7,5},{8,10},{9,11},{10,... | collective-permute-start | bytes 344072 | tf_op jit(solution)/shard_map/ppermute | solution.py:294
  6.9 5.3 %collective-permute-start.2 = (f32[2,112,128]{2,1,0:T(8,128)S(1)}, f32[2,112,128]{2,1,0:T(8,128)S(1)}, u32[]{:S(2)}, u32[]{:S(2)}) collective-permute-start(f32[2,112,128]{2,1,0:T(8,128)S(1)} %get-tuple-element.16), channel_id=1, source_target_pairs={{0,1},{1,0},{2,3},{3,2},{4,5},{5,4},{6,7},{7,6},{8,9},{9,8},{10,11... | collective-permute-start | bytes 344072 | tf_op jit(solution)/shard_map/ppermute | solution.py:294
  7.1 18.6 %collective-permute-start.5 = (f32[2,192,256]{2,1,0:T(8,128)S(1)}, f32[2,192,256]{2,1,0:T(8,128)S(1)}, u32[]{:S(2)}, u32[]{:S(2)}) collective-permute-start(f32[2,192,256]{2,1,0:T(8,128)S(1)} %get-tuple-element.17.refs_0_), channel_id=1, source_target_pairs={{0,16},{8,24},{16,0},{24,8},{1,17},{9,25},{17,1},{25,9},{2,18},{10... | collective-permute-start | bytes 1179656 | tf_op jit(solution)/shard_map/ppermute | solution.py:294
  9.0 16.7 %collective-permute-start.6 = (f32[2,192,256]{2,1,0:T(8,128)S(1)}, f32[2,192,256]{2,1,0:T(8,128)S(1)}, u32[]{:S(2)}, u32[]{:S(2)}) collective-permute-start(f32[2,192,256]{2,1,0:T(8,128)S(1)} %get-tuple-element.18), channel_id=1, source_target_pairs={{0,24},{8,16},{16,8},{24,0},{1,25},{9,17},{17,9},{25,1},{2,26},{10... | collective-permute-start | bytes 1179656 | tf_op jit(solution)/shard_map/ppermute | solution.py:294
  10.5 15.3 %collective-permute-start.4 = (f32[2,192,256]{2,1,0:T(8,128)S(1)}, f32[2,192,256]{2,1,0:T(8,128)S(1)}, u32[]{:S(2)}, u32[]{:S(2)}) collective-permute-start(f32[2,192,256]{2,1,0:T(8,128)S(1)} %get-tuple-element.18), channel_id=1, source_target_pairs={{0,8},{8,0},{16,24},{24,16},{1,9},{9,1},{17,25},{25,17},{2,10},{10... | collective-permute-start | bytes 1179656 | tf_op jit(solution)/shard_map/ppermute | solution.py:294
  12.3 7.7 %collective-permute-start.3 = (f32[2,112,128]{2,1,0:T(8,128)S(1)}, f32[2,112,128]{2,1,0:T(8,128)S(1)}, u32[]{:S(2)}, u32[]{:S(2)}) collective-permute-start(f32[2,112,128]{2,1,0:T(8,128)S(1)} %shard_map.38.sums), channel_id=1, source_target_pairs={{0,4},{1,5},{2,6},{3,7},{4,0},{5,1},{6,2},{7,3},{8,12},{9,13},{10,... | collective-permute-start | bytes 344072 | tf_op jit(solution)/shard_map/ppermute | solution.py:294
  21.4 10.4 %all-to-all-start = ((f32[16,2,8,128]{3,2,1,0:T(8,128)}), f32[16,2,8,128]{3,2,1,0:T(8,128)S(1)}, u32[]{:S(2)}, u32[]{:S(2)}) async-start(f32[16,2,8,128]{3,2,1,0:T(8,128)} %shard_map.39), calls=%async_computation | async-start | bytes 262144 | tf_op jit(solution)/shard_map/all_to_all | solution.py:330
  33.9 1.3 %collective-permute-start.7 = (f32[32,256]{1,0:T(8,128)S(1)}, f32[32,256]{1,0:T(8,128)S(1)}, u32[]{:S(2)}, u32[]{:S(2)}) collective-permute-start(f32[32,256]{1,0:T(8,128)S(1)} %shard_map.41.own), channel_id=1, source_target_pairs={{0,8},{8,0},{16,24},{24,16},{1,9},{9,1},{17,25},{25,17},{2,10},{10... | collective-permute-start | bytes 98312 | tf_op jit(solution)/shard_map/ppermute | solution.py:294

commit v5 on v4

--- a/solution.py
+++ b/solution.py
@@ -12,10 +12,6 @@
 VMEM = pl.BlockSpec(memory_space=pltpu.VMEM)
 SPAN = 4
 LIMIT = 48 * 1024 * 1024
-
-
-def pixel_place():
-    return lax.axis_index("high") * SPAN + lax.axis_index("low")
 
 
 def up(value, multiple):
@@ -104,17 +100,17 @@
     )
 
 
-def layout(rank, chunk):
+def layout(rank, chunk, chunks):
     rows = up(chunk, ROWS)
     whole, rest = divmod(pair_rows(rank) + rank, LANES)
     beside = LANES // rest if rest else 1
-    tail = -(-(rows // ROWS) // beside) if rest else 0
-    return rows, whole, rest, beside, rows * whole + ROWS * tail
+    tail = -(-(chunks * rows // ROWS) // beside) if rest else 0
+    return rows, whole, rest, beside, chunks * rows * whole + ROWS * tail
 
 
 def spec_kernel(flux_hbm, weights_hbm, basis_hbm, own, other, *rest, chunk, span):
     sends, scratch = rest[:span], rest[span:]
-    flux, weights, basis, twice, high, low, both, terms, last, grams, sems = scratch
+    flux, weights, basis, twice, high, low, both, terms, last, tails, grams, sems = scratch
     rank, pixels = basis.shape
     spectra = weights.shape[0]
     half = own.shape[2]
@@ -141,45 +137,46 @@
     both[0:spectra, :], both[spectra:, :] = halves(flux[...])
     part = dot(both[...], terms[...], 1)
     target = part[spectra:, 0:rank] + part[0:spectra, rank:] + part[0:spectra, 0:rank]
-    rows, whole, rest, beside, _ = layout(rank, chunk)
+    chunks = grams.shape[0] // span
+    rows, whole, rest, beside, _ = layout(rank, chunk, chunks)
     last[:, 0 : rest - rank] = packed[:, lead + rank - rest :]
     last[:, rest - rank : rest] = target
     for k in range(grams.shape[0]):
         for t in range(whole):
             grams[k, t * rows : t * rows + chunk, :] = packed[k * chunk : (k + 1) * chunk, t * LANES : (t + 1) * LANES]
-        for g in range(rows // ROWS):
-            base, count = rows * whole + g // beside * ROWS, min(ROWS, chunk - g * ROWS)
-            lanes = slice(g % beside * rest, (g % beside + 1) * rest)
-            grams[k, base : base + count, lanes] = last[k * chunk + g * ROWS : k * chunk + g * ROWS + count, 0:rest]
-    for k in range(grams.shape[0] // span):
-        for m, send in enumerate(sends):
-            send[k] = grams[pixel_place() ^ (span * k + m)]
+        tails[k, 0:chunk, 0:rest] = last[k * chunk : (k + 1) * chunk, 0:rest]
+    for m, send in enumerate(sends):
+        for h in range(chunks):
+            source = h * span + (lax.axis_index("low") ^ m)
+            send[h * whole * rows : (h + 1) * whole * rows, :] = grams[source, 0 : whole * rows, :]
+            for g in range(rows // ROWS):
+                slot = h * (rows // ROWS) + g
+                base = chunks * whole * rows + slot // beside * ROWS
+                lanes = slice(slot % beside * rest, (slot % beside + 1) * rest)
+                send[base : base + ROWS, lanes] = tails[source, g * ROWS : (g + 1) * ROWS, 0:rest]
     for copy in copies[3:]:
         copy.wait()
 
 
-def add_kernel(*refs, flip):
-    for h in range(refs[0].shape[0]):
-        total = refs[0][h]
-        for term in refs[1:-1]:
-            total = total + term[h ^ flip]
-        refs[-1][h] = total
-
-
-def coeff_kernel(sums, arrived, out, packed, full, scaled, *, rank, chunk):
-    chunks = sums.shape[0]
-    total = [sums[h] + arrived[h ^ (chunks // 2)] for h in range(chunks)]
-    rows, whole, rest, beside, _ = layout(rank, chunk)
+def add_kernel(*refs):
+    total = refs[0][...]
+    for term in refs[1:-1]:
+        total = total + term[...]
+    refs[-1][...] = total
+
+
+def coeff_kernel(sums, arrived, out, packed, full, scaled, *, rank, chunk, chunks):
+    total = sums[...] + arrived[...]
+    rows, whole, rest, beside, _ = layout(rank, chunk, chunks)
     filler = jnp.ones((LANES - chunks * rows, LANES), jnp.float32)
     for t in range(whole):
-        block = [total[h][t * rows : (t + 1) * rows] for h in range(chunks)]
+        block = [total[(h * whole + t) * rows : (h * whole + t + 1) * rows] for h in range(chunks)]
         packed[t * LANES : (t + 1) * LANES, :] = jnp.concatenate(block + [filler], axis=0).T
     groups = []
-    for h in range(chunks):
-        for g in range(rows // ROWS):
-            base = rows * whole + g // beside * ROWS
-            group = total[h][base : base + ROWS]
-            groups.append(pltpu.roll(group, LANES - g % beside * rest, 1) if g % beside else group)
+    for slot in range(chunks * rows // ROWS):
+        base = chunks * rows * whole + slot // beside * ROWS
+        group = total[base : base + ROWS]
+        groups.append(pltpu.roll(group, LANES - slot % beside * rest, 1) if slot % beside else group)
     packed[whole * LANES :, :] = jnp.concatenate(groups + [filler], axis=0).T
     lead = pair_rows(rank)
     unpack(packed, full, rank)
@@ -216,8 +213,7 @@
         columns = [jnp.zeros((ROWS, LANES), jnp.float32) for _ in range(width // LANES)]
         for q in range(peers):
             for k in range(group):
-                near = pixel_place() ^ k
-                part = tiles[q * SPAN + k % SPAN, near // SPAN]
+                part = tiles[q * SPAN + k % SPAN, k // SPAN]
                 start = q * spectra + k * chunk
                 shift = (start - a * chunk) % LANES
                 if shift:
@@ -285,7 +281,8 @@
     half, chunk = pixels // 2, spectra // groups
     lead = pair_rows(rank)
     wide = up(lead + rank, LANES)
-    rows = layout(rank, chunk)[-1]
+    chunks = groups // SPAN
+    kept = shape(layout(rank, chunk, chunks)[-1], LANES)
     half_type = jnp.bfloat16
     inputs = [pltpu.with_memory_space_constraint(a, pltpu.HBM) for a in (spectra_flux, pixel_weights, old_basis)]
 
@@ -295,7 +292,7 @@
 
     own, other, *sends = call(
         functools.partial(spec_kernel, chunk=chunk, span=SPAN),
-        [shape(2, spectra, half)] * 2 + [shape(groups // SPAN, rows, LANES)] * SPAN,
+        [shape(2, spectra, half)] * 2 + [kept] * SPAN,
         [
             (spectra, pixels),
             (spectra, pixels),
@@ -306,7 +303,8 @@
             (half_type, 2 * spectra, pixels),
             (half_type, 2 * rank, pixels),
             (spectra, LANES),
-            (groups, rows, LANES),
+            (groups, up(chunk, ROWS), LANES),
+            (groups, up(chunk, ROWS) * (wide // LANES), LANES),
             pltpu.SemaphoreType.DMA((7,)),
         ],
         *inputs,
@@ -314,14 +312,13 @@
     )
     arrived = [swap(sends[m], "pix", m) for m in range(SPAN - 1, 0, -1)]
     picks = [own] + [swap(other if q & 1 else own, "spec", q) for q in range(1, peers)]
-    kept = shape(*sends[0].shape)
-    sums = call(functools.partial(add_kernel, flip=0), kept, [], sends[0], *arrived)
+    sums = call(add_kernel, kept, [], sends[0], *arrived)
     reach = SPAN
     while 2 * reach < groups:
-        sums = call(functools.partial(add_kernel, flip=reach // SPAN), kept, [], sums, swap(sums, "pix", reach))
+        sums = call(add_kernel, kept, [], sums, swap(sums, "pix", reach))
         reach *= 2
     tiles = call(
-        functools.partial(coeff_kernel, rank=rank, chunk=chunk),
+        functools.partial(coeff_kernel, rank=rank, chunk=chunk, chunks=chunks),
         shape(peers * SPAN, groups // SPAN, ROWS, LANES),
         [(wide, LANES), (rank * rank, LANES), (rank * rank, LANES)],
         sums,

time: 36.1 us -> 35.7 us (0.989)
  no operation moved by 1% of the time
where the time goes in v5:
time: 35.7 us; the launch traced here: 35.4 us
  waiting for transfers between devices  14.8 us (41%)
  starting transfers between devices  13.7 us (38%)
  Pallas kernels  6.93 us (19%)
    ppermute x8, starting transfers between devices, swap(): return lax.ppermute(value, axis, [(s, s ^ mask) for s in range(size)])  9.42 us
    ppermute x8, waiting for transfers between devices, swap(): return lax.ppermute(value, axis, [(s, s ^ mask) for s in range(size)])  8.97 us
    pallas_call x6, Pallas kernels, call(): pl.pallas_call(kernel, out_shape=outs, in_specs=[pl.BlockSpec(memory_spac...  6.93 us
    all_to_all x1, waiting for transfers between devices, local(): tiles = lax.all_to_all(tiles, ('spec', 'low'), 0, 0)  5.8 us
    all_to_all x1, starting transfers between devices, local(): tiles = lax.all_to_all(tiles, ('spec', 'low'), 0, 0)  4.27 us
  transfers between devices with their start and end apart: 9, of which 5 were waited for; matrix products, arithmetic and copies ran while one was open for 0% of the time, Pallas kernels for 5%

profile of v5, /device:TPU:0, one launch (start us, length us, event | category | flops | bytes accessed | tf_op | source)
XLA Modules:
  0.0 35.4 jit_solution(1433864670642926599)
XLA Ops:
  0.0 2.5 %shard_map.37 = (f32[2,192,256]{2,1,0:T(8,128)S(1)}, f32[2,192,256]{2,1,0:T(8,128)S(1)}, f32[216,128]{1,0:T(8,128)S(1)}, f32[216,128]{1,0:T(8,128)S(1)}, f32[216,128]{1,0:T(8,128)S(1)}, /*index=5*/f32[216,128]{1,0:T(8,128)S(1)}) custom-call(f32[192,512]{1,0:T(8,128)} %flux_hbm.1, f32[192,512]{1,0:T(8,128)} %weights_hbm.1, f32[32,512]{1,0:T(8,128)} %basis_hbm.1), custom_call_target="tpu_custom_call" | custom-call | tf_op jit(solution)/shard_map/pallas_call | solution.py:264
  2.5 4.0 %collective-permute-start = (f32[216,128]{1,0:T(8,128)S(1)}, f32[216,128]{1,0:T(8,128)S(1)}, u32[]{:S(2)}, u32[]{:S(2)}) collective-permute-start(f32[216,128]{1,0:T(8,128)S(1)} %get-tuple-element.14), channel_id=1, source_target_pairs={{0,3},{1,2},{2,1},{3,0},{4,7},{5,6},{6,5},{7,4},{8,11},{9,10},{10,... | collective-permute-start | bytes 331784 | tf_op jit(solution)/shard_map/ppermute | solution.py:291
  6.5 0.5 %collective-permute-start.1 = (f32[216,128]{1,0:T(8,128)S(1)}, f32[216,128]{1,0:T(8,128)S(1)}, u32[]{:S(2)}, u32[]{:S(2)}) collective-permute-start(f32[216,128]{1,0:T(8,128)S(1)} %get-tuple-element.15), channel_id=1, source_target_pairs={{0,2},{1,3},{2,0},{3,1},{4,6},{5,7},{6,4},{7,5},{8,10},{9,11},{10,... | collective-permute-start | bytes 331784 | tf_op jit(solution)/shard_map/ppermute | solution.py:291
  7.0 0.2 collective-permute-start.2
  7.1 1.9 %collective-permute-start.5 = (f32[2,192,256]{2,1,0:T(8,128)S(1)}, f32[2,192,256]{2,1,0:T(8,128)S(1)}, u32[]{:S(2)}, u32[]{:S(2)}) collective-permute-start(f32[2,192,256]{2,1,0:T(8,128)S(1)} %get-tuple-element.17.refs_0_), channel_id=1, source_target_pairs={{0,16},{8,24},{16,0},{24,8},{1,17},{9,25},{17,1},{25,9},{2,18},{10... | collective-permute-start | bytes 1179656 | tf_op jit(solution)/shard_map/ppermute | solution.py:291
  9.0 0.0 collective-permute-start.6
  9.0 1.4 %collective-permute-done.refs_1_ = f32[216,128]{1,0:T(8,128)S(1)} collective-permute-done((f32[216,128]{1,0:T(8,128)S(1)}, f32[216,128]{1,0:T(8,128)S(1)}, u32[]{:S(2)}, u32[]{:S(2)}) %collective-permute-start) | collective-permute-done | bytes 110624 | tf_op jit(solution)/shard_map/ppermute | solution.py:291
  10.4 0.0 collective-permute-start.4
  10.4 1.7 %collective-permute-done.1.refs_2_ = f32[216,128]{1,0:T(8,128)S(1)} collective-permute-done((f32[216,128]{1,0:T(8,128)S(1)}, f32[216,128]{1,0:T(8,128)S(1)}, u32[]{:S(2)}, u32[]{:S(2)}) %collective-permute-start.1) | collective-permute-done | bytes 110624 | tf_op jit(solution)/shard_map/ppermute | solution.py:291
  12.1 0.0 collective-permute-done.2.refs_3_
  12.1 2.7 %collective-permute-start.3 = (f32[216,128]{1,0:T(8,128)S(1)}, f32[216,128]{1,0:T(8,128)S(1)}, u32[]{:S(2)}, u32[]{:S(2)}) collective-permute-start(f32[216,128]{1,0:T(8,128)S(1)} %shard_map.38.sums), channel_id=1, source_target_pairs={{0,4},{1,5},{2,6},{3,7},{4,0},{5,1},{6,2},{7,3},{8,12},{9,13},{10,... | collective-permute-start | bytes 331784 | tf_op jit(solution)/shard_map/ppermute | solution.py:291
  14.8 4.8 %collective-permute-done.3.arrived = f32[216,128]{1,0:T(8,128)S(1)} collective-permute-done((f32[216,128]{1,0:T(8,128)S(1)}, f32[216,128]{1,0:T(8,128)S(1)}, u32[]{:S(2)}, u32[]{:S(2)}) %collective-permute-start.3) | collective-permute-done | bytes 110624 | tf_op jit(solution)/shard_map/ppermute | solution.py:291
  19.6 1.4 %shard_map.39 = f32[16,2,8,128]{3,2,1,0:T(8,128)} custom-call(f32[216,128]{1,0:T(8,128)S(1)} %shard_map.38.sums, f32[216,128]{1,0:T(8,128)S(1)} %collective-permute-done.3.arrived), custom_call_target="tpu_custom_call" | custom-call | tf_op jit(solution)/shard_map/pallas_call | solution.py:264
  21.1 4.3 %all-to-all-start = ((f32[16,2,8,128]{3,2,1,0:T(8,128)}), f32[16,2,8,128]{3,2,1,0:T(8,128)S(1)}, u32[]{:S(2)}, u32[]{:S(2)}) async-start(f32[16,2,8,128]{3,2,1,0:T(8,128)} %shard_map.39), calls=%async_computation | async-start | bytes 262144 | tf_op jit(solution)/shard_map/all_to_all | solution.py:327
  25.3 0.0 collective-permute-done.5.refs_2_
  25.4 0.0 collective-permute-done.6.refs_3_
  25.4 0.0 collective-permute-done.4.refs_1_
  25.4 0.2 shard_map.40
  25.6 5.8 %all-to-all-done.tiles = f32[16,2,8,128]{3,2,1,0:T(8,128)S(1)} async-done(((f32[16,2,8,128]{3,2,1,0:T(8,128)}), f32[16,2,8,128]{3,2,1,0:T(8,128)S(1)}, u32[]{:S(2)}, u32[]{:S(2)}) %all-to-all-start) | async-done | bytes 131104 | tf_op jit(solution)/shard_map/all_to_all | solution.py:327
  31.4 2.1 %shard_map.41.own = f32[32,256]{1,0:T(8,128)S(1)} custom-call(f32[16,2,8,128]{3,2,1,0:T(8,128)S(1)} %all-to-all-done.tiles, bf16[2,768,256]{2,1,0:T(8,128)(2,1)S(1)} %get-tuple-element.19.high, bf16[2,768,256]{2,1,0:T(8,128)(2,1)S(1)} %get-tuple-element.20.low), custom_call_target="tpu_custom_call" | custom-call | tf_op jit(solution)/shard_map/pallas_call | solution.py:264
  33.5 0.2 collective-permute-start.7
  33.7 1.1 %collective-permute-done.7.other = f32[32,256]{1,0:T(8,128)S(1)} collective-permute-done((f32[32,256]{1,0:T(8,128)S(1)}, f32[32,256]{1,0:T(8,128)S(1)}, u32[]{:S(2)}, u32[]{:S(2)}) %collective-permute-start.7) | collective-permute-done | bytes 32800 | tf_op jit(solution)/shard_map/ppermute | solution.py:291
  34.8 0.6 %shard_map.42 = f32[32,512]{1,0:T(8,128)} custom-call(f32[32,256]{1,0:T(8,128)S(1)} %shard_map.41.own, f32[32,256]{1,0:T(8,128)S(1)} %collective-permute-done.7.other), custom_call_target="tpu_custom_call" | custom-call | tf_op jit(solution)/shard_map/pallas_call | solution.py:264
  (1 shorter events, 0.0 us)
Async XLA Ops:
  2.5 7.9 %collective-permute-start = (f32[216,128]{1,0:T(8,128)S(1)}, f32[216,128]{1,0:T(8,128)S(1)}, u32[]{:S(2)}, u32[]{:S(2)}) collective-permute-start(f32[216,128]{1,0:T(8,128)S(1)} %get-tuple-element.14), channel_id=1, source_target_pairs={{0,3},{1,2},{2,1},{3,0},{4,7},{5,6},{6,5},{7,4},{8,11},{9,10},{10,... | collective-permute-start | bytes 331784 | tf_op jit(solution)/shard_map/ppermute | solution.py:291
  6.5 5.6 %collective-permute-start.1 = (f32[216,128]{1,0:T(8,128)S(1)}, f32[216,128]{1,0:T(8,128)S(1)}, u32[]{:S(2)}, u32[]{:S(2)}) collective-permute-start(f32[216,128]{1,0:T(8,128)S(1)} %get-tuple-element.15), channel_id=1, source_target_pairs={{0,2},{1,3},{2,0},{3,1},{4,6},{5,7},{6,4},{7,5},{8,10},{9,11},{10,... | collective-permute-start | bytes 331784 | tf_op jit(solution)/shard_map/ppermute | solution.py:291
  7.0 5.1 %collective-permute-start.2 = (f32[216,128]{1,0:T(8,128)S(1)}, f32[216,128]{1,0:T(8,128)S(1)}, u32[]{:S(2)}, u32[]{:S(2)}) collective-permute-start(f32[216,128]{1,0:T(8,128)S(1)} %get-tuple-element.16), channel_id=1, source_target_pairs={{0,1},{1,0},{2,3},{3,2},{4,5},{5,4},{6,7},{7,6},{8,9},{9,8},{10,11... | collective-permute-start | bytes 331784 | tf_op jit(solution)/shard_map/ppermute | solution.py:291
  7.1 18.2 %collective-permute-start.5 = (f32[2,192,256]{2,1,0:T(8,128)S(1)}, f32[2,192,256]{2,1,0:T(8,128)S(1)}, u32[]{:S(2)}, u32[]{:S(2)}) collective-permute-start(f32[2,192,256]{2,1,0:T(8,128)S(1)} %get-tuple-element.17.refs_0_), channel_id=1, source_target_pairs={{0,16},{8,24},{16,0},{24,8},{1,17},{9,25},{17,1},{25,9},{2,18},{10... | collective-permute-start | bytes 1179656 | tf_op jit(solution)/shard_map/ppermute | solution.py:291
  9.0 16.4 %collective-permute-start.6 = (f32[2,192,256]{2,1,0:T(8,128)S(1)}, f32[2,192,256]{2,1,0:T(8,128)S(1)}, u32[]{:S(2)}, u32[]{:S(2)}) collective-permute-start(f32[2,192,256]{2,1,0:T(8,128)S(1)} %get-tuple-element.18), channel_id=1, source_target_pairs={{0,24},{8,16},{16,8},{24,0},{1,25},{9,17},{17,9},{25,1},{2,26},{10... | collective-permute-start | bytes 1179656 | tf_op jit(solution)/shard_map/ppermute | solution.py:291
  10.4 15.0 %collective-permute-start.4 = (f32[2,192,256]{2,1,0:T(8,128)S(1)}, f32[2,192,256]{2,1,0:T(8,128)S(1)}, u32[]{:S(2)}, u32[]{:S(2)}) collective-permute-start(f32[2,192,256]{2,1,0:T(8,128)S(1)} %get-tuple-element.18), channel_id=1, source_target_pairs={{0,8},{8,0},{16,24},{24,16},{1,9},{9,1},{17,25},{25,17},{2,10},{10... | collective-permute-start | bytes 1179656 | tf_op jit(solution)/shard_map/ppermute | solution.py:291
  12.1 7.5 %collective-permute-start.3 = (f32[216,128]{1,0:T(8,128)S(1)}, f32[216,128]{1,0:T(8,128)S(1)}, u32[]{:S(2)}, u32[]{:S(2)}) collective-permute-start(f32[216,128]{1,0:T(8,128)S(1)} %shard_map.38.sums), channel_id=1, source_target_pairs={{0,4},{1,5},{2,6},{3,7},{4,0},{5,1},{6,2},{7,3},{8,12},{9,13},{10,... | collective-permute-start | bytes 331784 | tf_op jit(solution)/shard_map/ppermute | solution.py:291
  21.1 10.4 %all-to-all-start = ((f32[16,2,8,128]{3,2,1,0:T(8,128)}), f32[16,2,8,128]{3,2,1,0:T(8,128)S(1)}, u32[]{:S(2)}, u32[]{:S(2)}) async-start(f32[16,2,8,128]{3,2,1,0:T(8,128)} %shard_map.39), calls=%async_computation | async-start | bytes 262144 | tf_op jit(solution)/shard_map/all_to_all | solution.py:327
  33.5 1.3 %collective-permute-start.7 = (f32[32,256]{1,0:T(8,128)S(1)}, f32[32,256]{1,0:T(8,128)S(1)}, u32[]{:S(2)}, u32[]{:S(2)}) collective-permute-start(f32[32,256]{1,0:T(8,128)S(1)} %shard_map.41.own), channel_id=1, source_target_pairs={{0,8},{8,0},{16,24},{24,16},{1,9},{9,1},{17,25},{25,17},{2,10},{10... | collective-permute-start | bytes 98312 | tf_op jit(solution)/shard_map/ppermute | solution.py:291

commit v6 on v5

--- a/solution.py
+++ b/solution.py
@@ -310,7 +310,7 @@
         *inputs,
         space=pl.ANY,
     )
-    arrived = [swap(sends[m], "pix", m) for m in range(SPAN - 1, 0, -1)]
+    arrived = [swap(sends[m], "pix", m) for m in sorted(range(1, SPAN), key=lambda m: (1 - m % 2, m))]
     picks = [own] + [swap(other if q & 1 else own, "spec", q) for q in range(1, peers)]
     sums = call(add_kernel, kept, [], sends[0], *arrived)
     reach = SPAN

time: 35.7 us -> 35.5 us (level)
  transfers between devices with their start and end apart: 9 -> 9, of which waited for: 5 -> 6; matrix products, arithmetic and copies ran while one was open for 0% -> 0% of each run, Pallas kernels for 5% -> 5%
where the time goes in v6:
time: 35.5 us; the launch traced here: 35.3 us
  waiting for transfers between devices  14.7 us (41%)
  starting transfers between devices  13.6 us (38%)
  Pallas kernels  6.93 us (20%)
    ppermute x8, starting transfers between devices, swap(): return lax.ppermute(value, axis, [(s, s ^ mask) for s in range(size)])  9.57 us
    ppermute x8, waiting for transfers between devices, swap(): return lax.ppermute(value, axis, [(s, s ^ mask) for s in range(size)])  8.91 us
    pallas_call x6, Pallas kernels, call(): pl.pallas_call(kernel, out_shape=outs, in_specs=[pl.BlockSpec(memory_spac...  6.93 us
    all_to_all x1, waiting for transfers between devices, local(): tiles = lax.all_to_all(tiles, ('spec', 'low'), 0, 0)  5.8 us
    all_to_all x1, starting transfers between devices, local(): tiles = lax.all_to_all(tiles, ('spec', 'low'), 0, 0)  4.02 us
  transfers between devices with their start and end apart: 9, of which 6 were waited for; matrix products, arithmetic and copies ran while one was open for 0% of the time, Pallas kernels for 5%

profile of v6, /device:TPU:0, one launch (start us, length us, event | category | flops | bytes accessed | tf_op | source)
XLA Modules:
  0.0 35.3 jit_solution(464256503867762699)
XLA Ops:
  0.0 2.5 %shard_map.37 = (f32[2,192,256]{2,1,0:T(8,128)S(1)}, f32[2,192,256]{2,1,0:T(8,128)S(1)}, f32[216,128]{1,0:T(8,128)S(1)}, f32[216,128]{1,0:T(8,128)S(1)}, f32[216,128]{1,0:T(8,128)S(1)}, /*index=5*/f32[216,128]{1,0:T(8,128)S(1)}) custom-call(f32[192,512]{1,0:T(8,128)} %flux_hbm.1, f32[192,512]{1,0:T(8,128)} %weights_hbm.1, f32[32,512]{1,0:T(8,128)} %basis_hbm.1), custom_call_target="tpu_custom_call" | custom-call | tf_op jit(solution)/shard_map/pallas_call | solution.py:264
  2.5 3.0 %collective-permute-start = (f32[216,128]{1,0:T(8,128)S(1)}, f32[216,128]{1,0:T(8,128)S(1)}, u32[]{:S(2)}, u32[]{:S(2)}) collective-permute-start(f32[216,128]{1,0:T(8,128)S(1)} %get-tuple-element.14), channel_id=1, source_target_pairs={{0,1},{1,0},{2,3},{3,2},{4,5},{5,4},{6,7},{7,6},{8,9},{9,8},{10,11... | collective-permute-start | bytes 331784 | tf_op jit(solution)/shard_map/ppermute | solution.py:291
  5.5 1.5 %collective-permute-start.1 = (f32[216,128]{1,0:T(8,128)S(1)}, f32[216,128]{1,0:T(8,128)S(1)}, u32[]{:S(2)}, u32[]{:S(2)}) collective-permute-start(f32[216,128]{1,0:T(8,128)S(1)} %get-tuple-element.15), channel_id=1, source_target_pairs={{0,3},{1,2},{2,1},{3,0},{4,7},{5,6},{6,5},{7,4},{8,11},{9,10},{10,... | collective-permute-start | bytes 331784 | tf_op jit(solution)/shard_map/ppermute | solution.py:291
  7.0 0.0 collective-permute-start.2
  7.1 1.9 %collective-permute-start.5 = (f32[2,192,256]{2,1,0:T(8,128)S(1)}, f32[2,192,256]{2,1,0:T(8,128)S(1)}, u32[]{:S(2)}, u32[]{:S(2)}) collective-permute-start(f32[2,192,256]{2,1,0:T(8,128)S(1)} %get-tuple-element.17.refs_0_), channel_id=1, source_target_pairs={{0,16},{8,24},{16,0},{24,8},{1,17},{9,25},{17,1},{25,9},{2,18},{10... | collective-permute-start | bytes 1179656 | tf_op jit(solution)/shard_map/ppermute | solution.py:291
  9.0 0.0 collective-permute-start.6
  9.0 1.2 %collective-permute-done.refs_1_ = f32[216,128]{1,0:T(8,128)S(1)} collective-permute-done((f32[216,128]{1,0:T(8,128)S(1)}, f32[216,128]{1,0:T(8,128)S(1)}, u32[]{:S(2)}, u32[]{:S(2)}) %collective-permute-start) | collective-permute-done | bytes 110624 | tf_op jit(solution)/shard_map/ppermute | solution.py:291
  10.2 0.0 collective-permute-start.4
  10.2 2.0 %collective-permute-done.1.refs_2_ = f32[216,128]{1,0:T(8,128)S(1)} collective-permute-done((f32[216,128]{1,0:T(8,128)S(1)}, f32[216,128]{1,0:T(8,128)S(1)}, u32[]{:S(2)}, u32[]{:S(2)}) %collective-permute-start.1) | collective-permute-done | bytes 110624 | tf_op jit(solution)/shard_map/ppermute | solution.py:291
  12.2 0.1 collective-permute-done.2.refs_3_
  12.3 2.9 %collective-permute-start.3 = (f32[216,128]{1,0:T(8,128)S(1)}, f32[216,128]{1,0:T(8,128)S(1)}, u32[]{:S(2)}, u32[]{:S(2)}) collective-permute-start(f32[216,128]{1,0:T(8,128)S(1)} %shard_map.38.sums), channel_id=1, source_target_pairs={{0,4},{1,5},{2,6},{3,7},{4,0},{5,1},{6,2},{7,3},{8,12},{9,13},{10,... | collective-permute-start | bytes 331784 | tf_op jit(solution)/shard_map/ppermute | solution.py:291
  15.1 4.6 %collective-permute-done.3.arrived = f32[216,128]{1,0:T(8,128)S(1)} collective-permute-done((f32[216,128]{1,0:T(8,128)S(1)}, f32[216,128]{1,0:T(8,128)S(1)}, u32[]{:S(2)}, u32[]{:S(2)}) %collective-permute-start.3) | collective-permute-done | bytes 110624 | tf_op jit(solution)/shard_map/ppermute | solution.py:291
  19.7 1.4 %shard_map.39 = f32[16,2,8,128]{3,2,1,0:T(8,128)} custom-call(f32[216,128]{1,0:T(8,128)S(1)} %shard_map.38.sums, f32[216,128]{1,0:T(8,128)S(1)} %collective-permute-done.3.arrived), custom_call_target="tpu_custom_call" | custom-call | tf_op jit(solution)/shard_map/pallas_call | solution.py:264
  21.2 4.0 %all-to-all-start = ((f32[16,2,8,128]{3,2,1,0:T(8,128)}), f32[16,2,8,128]{3,2,1,0:T(8,128)S(1)}, u32[]{:S(2)}, u32[]{:S(2)}) async-start(f32[16,2,8,128]{3,2,1,0:T(8,128)} %shard_map.39), calls=%async_computation | async-start | bytes 262144 | tf_op jit(solution)/shard_map/all_to_all | solution.py:327
  25.2 0.0 collective-permute-done.5.refs_2_
  25.2 0.0 collective-permute-done.6.refs_3_
  25.2 0.0 collective-permute-done.4.refs_1_
  25.2 0.2 shard_map.40
  25.5 5.8 %all-to-all-done.tiles = f32[16,2,8,128]{3,2,1,0:T(8,128)S(1)} async-done(((f32[16,2,8,128]{3,2,1,0:T(8,128)}), f32[16,2,8,128]{3,2,1,0:T(8,128)S(1)}, u32[]{:S(2)}, u32[]{:S(2)}) %all-to-all-start) | async-done | bytes 131104 | tf_op jit(solution)/shard_map/all_to_all | solution.py:327
  31.3 2.1 %shard_map.41.own = f32[32,256]{1,0:T(8,128)S(1)} custom-call(f32[16,2,8,128]{3,2,1,0:T(8,128)S(1)} %all-to-all-done.tiles, bf16[2,768,256]{2,1,0:T(8,128)(2,1)S(1)} %get-tuple-element.19.high, bf16[2,768,256]{2,1,0:T(8,128)(2,1)S(1)} %get-tuple-element.20.low), custom_call_target="tpu_custom_call" | custom-call | tf_op jit(solution)/shard_map/pallas_call | solution.py:264
  33.4 0.2 collective-permute-start.7
  33.6 1.1 %collective-permute-done.7.other = f32[32,256]{1,0:T(8,128)S(1)} collective-permute-done((f32[32,256]{1,0:T(8,128)S(1)}, f32[32,256]{1,0:T(8,128)S(1)}, u32[]{:S(2)}, u32[]{:S(2)}) %collective-permute-start.7) | collective-permute-done | bytes 32800 | tf_op jit(solution)/shard_map/ppermute | solution.py:291
  34.7 0.6 %shard_map.42 = f32[32,512]{1,0:T(8,128)} custom-call(f32[32,256]{1,0:T(8,128)S(1)} %shard_map.41.own, f32[32,256]{1,0:T(8,128)S(1)} %collective-permute-done.7.other), custom_call_target="tpu_custom_call" | custom-call | tf_op jit(solution)/shard_map/pallas_call | solution.py:264
  (1 shorter events, 0.0 us)
Async XLA Ops:
  2.5 7.7 %collective-permute-start = (f32[216,128]{1,0:T(8,128)S(1)}, f32[216,128]{1,0:T(8,128)S(1)}, u32[]{:S(2)}, u32[]{:S(2)}) collective-permute-start(f32[216,128]{1,0:T(8,128)S(1)} %get-tuple-element.14), channel_id=1, source_target_pairs={{0,1},{1,0},{2,3},{3,2},{4,5},{5,4},{6,7},{7,6},{8,9},{9,8},{10,11... | collective-permute-start | bytes 331784 | tf_op jit(solution)/shard_map/ppermute | solution.py:291
  5.5 6.7 %collective-permute-start.1 = (f32[216,128]{1,0:T(8,128)S(1)}, f32[216,128]{1,0:T(8,128)S(1)}, u32[]{:S(2)}, u32[]{:S(2)}) collective-permute-start(f32[216,128]{1,0:T(8,128)S(1)} %get-tuple-element.15), channel_id=1, source_target_pairs={{0,3},{1,2},{2,1},{3,0},{4,7},{5,6},{6,5},{7,4},{8,11},{9,10},{10,... | collective-permute-start | bytes 331784 | tf_op jit(solution)/shard_map/ppermute | solution.py:291
  7.0 5.2 %collective-permute-start.2 = (f32[216,128]{1,0:T(8,128)S(1)}, f32[216,128]{1,0:T(8,128)S(1)}, u32[]{:S(2)}, u32[]{:S(2)}) collective-permute-start(f32[216,128]{1,0:T(8,128)S(1)} %get-tuple-element.16), channel_id=1, source_target_pairs={{0,2},{1,3},{2,0},{3,1},{4,6},{5,7},{6,4},{7,5},{8,10},{9,11},{10,... | collective-permute-start | bytes 331784 | tf_op jit(solution)/shard_map/ppermute | solution.py:291
  7.1 18.1 %collective-permute-start.5 = (f32[2,192,256]{2,1,0:T(8,128)S(1)}, f32[2,192,256]{2,1,0:T(8,128)S(1)}, u32[]{:S(2)}, u32[]{:S(2)}) collective-permute-start(f32[2,192,256]{2,1,0:T(8,128)S(1)} %get-tuple-element.17.refs_0_), channel_id=1, source_target_pairs={{0,16},{8,24},{16,0},{24,8},{1,17},{9,25},{17,1},{25,9},{2,18},{10... | collective-permute-start | bytes 1179656 | tf_op jit(solution)/shard_map/ppermute | solution.py:291
  9.0 16.2 %collective-permute-start.6 = (f32[2,192,256]{2,1,0:T(8,128)S(1)}, f32[2,192,256]{2,1,0:T(8,128)S(1)}, u32[]{:S(2)}, u32[]{:S(2)}) collective-permute-start(f32[2,192,256]{2,1,0:T(8,128)S(1)} %get-tuple-element.18), channel_id=1, source_target_pairs={{0,24},{8,16},{16,8},{24,0},{1,25},{9,17},{17,9},{25,1},{2,26},{10... | collective-permute-start | bytes 1179656 | tf_op jit(solution)/shard_map/ppermute | solution.py:291
  10.2 15.0 %collective-permute-start.4 = (f32[2,192,256]{2,1,0:T(8,128)S(1)}, f32[2,192,256]{2,1,0:T(8,128)S(1)}, u32[]{:S(2)}, u32[]{:S(2)}) collective-permute-start(f32[2,192,256]{2,1,0:T(8,128)S(1)} %get-tuple-element.18), channel_id=1, source_target_pairs={{0,8},{8,0},{16,24},{24,16},{1,9},{9,1},{17,25},{25,17},{2,10},{10... | collective-permute-start | bytes 1179656 | tf_op jit(solution)/shard_map/ppermute | solution.py:291
  12.3 7.4 %collective-permute-start.3 = (f32[216,128]{1,0:T(8,128)S(1)}, f32[216,128]{1,0:T(8,128)S(1)}, u32[]{:S(2)}, u32[]{:S(2)}) collective-permute-start(f32[216,128]{1,0:T(8,128)S(1)} %shard_map.38.sums), channel_id=1, source_target_pairs={{0,4},{1,5},{2,6},{3,7},{4,0},{5,1},{6,2},{7,3},{8,12},{9,13},{10,... | collective-permute-start | bytes 331784 | tf_op jit(solution)/shard_map/ppermute | solution.py:291
  21.2 10.1 %all-to-all-start = ((f32[16,2,8,128]{3,2,1,0:T(8,128)}), f32[16,2,8,128]{3,2,1,0:T(8,128)S(1)}, u32[]{:S(2)}, u32[]{:S(2)}) async-start(f32[16,2,8,128]{3,2,1,0:T(8,128)} %shard_map.39), calls=%async_computation | async-start | bytes 262144 | tf_op jit(solution)/shard_map/all_to_all | solution.py:327
  33.4 1.3 %collective-permute-start.7 = (f32[32,256]{1,0:T(8,128)S(1)}, f32[32,256]{1,0:T(8,128)S(1)}, u32[]{:S(2)}, u32[]{:S(2)}) collective-permute-start(f32[32,256]{1,0:T(8,128)S(1)} %shard_map.41.own), channel_id=1, source_target_pairs={{0,8},{8,0},{16,24},{24,16},{1,9},{9,1},{17,25},{25,17},{2,10},{10... | collective-permute-start | bytes 98312 | tf_op jit(solution)/shard_map/ppermute | solution.py:291
